TPU v7x, 32 devices: a whole 2x2x4 slice. The times are simulated.
32 devices in a mesh: grp: 2 (over y), gx: 4 (over z), gy: 4 (over x, core).
Axes of the slice: x: 2, y: 2, z: 4, core: 2. Of those that a mesh axis runs over, the one named last changes fastest.
Arguments:
- plane_input: bfloat16 [64, 256, 2048], P(None, ('grp', 'gx'), 'gy'), parts along dimension 1, may hold values from -6 to 6
- row_weight: bfloat16 [2, 16, 64, 64], replicated, may hold values from -0.75 to 0.75
- col_weight: bfloat16 [2, 16, 64, 64], replicated, may hold values from -0.75 to 0.75
- skip_weight: bfloat16 [64, 64], replicated, may hold values from -0.75 to 0.75
- up_weight: bfloat16 [64, 256], replicated, may hold values from -0.03491211 to 0.03491211
- up_bias: float32 [256], replicated, may hold values from -3 to -2
- down_weight: bfloat16 [256, 64], replicated, may hold values from -1.5 to 1.5
- down_bias: float32 [64], replicated, may hold values from -0.15 to 0.15
Outputs:
- output: bfloat16 [64, 256, 2048], P(None, ('grp', 'gx'), 'gy'), parts along dimension 1
There are 2 independent parts, one for each index of `grp`. A program takes and returns all parts, laid end to end along the dimension named above; an argument that names none is the same for every part. Nothing has to cross between parts.
All inputs are finite; a program needn't handle non-finite values.
Results may differ from a plain program's by a relative error of at most 0.0066.
Values may be sent and summed in bfloat16 or wider, within the bound.
No kernel may reach another device: no remote copies, remote signals or barrier semaphores. Data moves between devices by JAX's collectives and lax.ppermute only.
A program may use at most 128 MiB of HBM per device.

v0:
```python
import math

import jax
import jax.numpy as jnp
from jax import lax
from jax.sharding import PartitionSpec as P


def forward_table(mode_count, period, offset, number):
    wave_index = jnp.arange(mode_count, dtype=jnp.int32)
    cell_index = offset + jnp.arange(number, dtype=jnp.int32)
    phases = wave_index[:, None] * cell_index[None, :] % period
    angles = phases.astype(jnp.float32) * (2.0 * math.pi / period)
    return jnp.concatenate([jnp.cos(angles), -jnp.sin(angles)], axis=0).astype(jnp.bfloat16)


def inverse_table(mode_count, period, offset, number):
    wave_index = jnp.arange(mode_count, dtype=jnp.int32)
    cell_index = offset + jnp.arange(number, dtype=jnp.int32)
    phases = cell_index[:, None] * wave_index[None, :] % period
    angles = phases.astype(jnp.float32) * (2.0 * math.pi / period)
    factors = jnp.where(wave_index == 0, 1.0, 2.0).astype(jnp.float32)[None, :]
    return jnp.concatenate([factors * jnp.cos(angles), -factors * jnp.sin(angles)], axis=1).astype(
        jnp.bfloat16
    )


def mix_rows(spectrum, weight):
    mode_count = weight.shape[1]
    highest = lax.Precision.HIGHEST
    real_part = spectrum[:, :mode_count]
    imag_part = spectrum[:, mode_count:]
    w_real = weight[0].astype(jnp.float32)
    w_imag = weight[1].astype(jnp.float32)
    first = jnp.einsum("cky,kco->oky", real_part, w_real, precision=highest) - jnp.einsum(
        "cky,kco->oky", imag_part, w_imag, precision=highest
    )
    second = jnp.einsum("cky,kco->oky", imag_part, w_real, precision=highest) + jnp.einsum(
        "cky,kco->oky", real_part, w_imag, precision=highest
    )
    return jnp.concatenate([first, second], axis=1).astype(jnp.bfloat16)


def mix_cols(spectrum, weight):
    mode_count = weight.shape[1]
    highest = lax.Precision.HIGHEST
    real_part = spectrum[:, :, :mode_count]
    imag_part = spectrum[:, :, mode_count:]
    w_real = weight[0].astype(jnp.float32)
    w_imag = weight[1].astype(jnp.float32)
    first = jnp.einsum("cxk,kco->oxk", real_part, w_real, precision=highest) - jnp.einsum(
        "cxk,kco->oxk", imag_part, w_imag, precision=highest
    )
    second = jnp.einsum("cxk,kco->oxk", imag_part, w_real, precision=highest) + jnp.einsum(
        "cxk,kco->oxk", real_part, w_imag, precision=highest
    )
    return jnp.concatenate([first, second], axis=2).astype(jnp.bfloat16)


def body(
    plane_input, row_weight, col_weight, skip_weight, up_weight, up_bias, down_weight, down_bias
):
    mode_count = row_weight.shape[1]
    row_count = plane_input.shape[1]
    col_count = plane_input.shape[2]
    row_total = row_count * lax.axis_size("gx")
    col_total = col_count * lax.axis_size("gy")
    row_offset = lax.axis_index("gx") * row_count
    col_offset = lax.axis_index("gy") * col_count
    row_forward = forward_table(mode_count, row_total, row_offset, row_count)
    col_forward = forward_table(mode_count, col_total, col_offset, col_count)
    row_inverse = inverse_table(mode_count, row_total, row_offset, row_count)
    col_inverse = inverse_table(mode_count, col_total, col_offset, col_count)
    row_scale = float(row_total * mode_count) ** (-0.5)
    col_scale = float(col_total * mode_count) ** (-0.5)
    row_partial = jnp.einsum(
        "cxy,jx->cjy", plane_input, row_forward, preferred_element_type=jnp.float32
    )
    col_partial = jnp.einsum(
        "cxy,jy->cxj", plane_input, col_forward, preferred_element_type=jnp.float32
    )
    row_share = lax.psum_scatter(row_partial, "gx", scatter_dimension=2, tiled=True)
    from_rows = (
        jnp.einsum(
            "ojy,xj->oxy",
            lax.all_gather(mix_rows(row_share, row_weight), "gx", axis=2, tiled=True),
            row_inverse,
            preferred_element_type=jnp.float32,
        )
        * row_scale
    )
    col_spectrum = lax.psum(col_partial, "gy")
    from_cols = (
        jnp.einsum(
            "oxj,yj->oxy",
            mix_cols(col_spectrum, col_weight),
            col_inverse,
            preferred_element_type=jnp.float32,
        )
        * col_scale
    )
    local = jnp.einsum("cxy,co->oxy", plane_input, skip_weight, preferred_element_type=jnp.float32)
    mixed_input = (from_rows + from_cols + local).astype(jnp.bfloat16)
    hidden_pre = (
        jnp.einsum("cxy,ch->hxy", mixed_input, up_weight, preferred_element_type=jnp.float32)
        + up_bias[:, None, None]
    )
    hidden = jax.nn.gelu(hidden_pre, approximate=False).astype(jnp.bfloat16)
    result = (
        jnp.einsum("hxy,ho->oxy", hidden, down_weight, preferred_element_type=jnp.float32)
        + down_bias[:, None, None]
    )
    return result.astype(jnp.bfloat16)


def solution(mesh):
    placed = (P(None, ("grp", "gx"), "gy"), P(), P(), P(), P(), P(), P(), P())
    return jax.shard_map(
        body, mesh=mesh, in_specs=placed, out_specs=P(None, ("grp", "gx"), "gy"), check_vma=False
    )
```

profile of v0, /device:TPU:0, one launch (start us, length us, event | category | flops | bytes accessed | tf_op | source)
XLA Modules:
  0.0 221.4 jit_solution(16593051166793812107)
XLA Ops:
  7.4 0.0 copy-start
  7.4 0.0 reduce-scatter.2.cloned.1.call-start
  7.4 0.1 cosine_convert_fusion.1
  7.4 1.5 copy-done
  9.0 2.6 %convolution_bitcast_fusion = f32[64,32,512]{2,1,0:T(8,128)} fusion(bf16[64,32,512]{2,1,0:T(8,128)(2,1)S(1)} %copy-done, bf16[16,32]{1,0:T(8,128)(2,1)S(1)} %get-tuple-element.16, bf16[16,32]{1,0:T(8,128)(2,1)S(1)} %get-tuple-element.15), kind=kOutput, calls=%fused_computation.29 | convolution fusion | flops 67112960 | bytes 6293504 | tf_op jit(solution)/shard_map/cxy,jx->cjy/dot_general | solution.py:76
  11.6 0.0 copy-start.2
  11.6 0.0 reduce-scatter.2.cloned.1.call-update
  11.6 0.0 all-reduce.2.cloned.1.call-start
  11.7 0.1 cosine_convert_fusion
  11.8 3.2 %fusion.30 = f32[64,32,32]{0,2,1:T(8,128)} fusion(bf16[64,32,512]{2,1,0:T(8,128)(2,1)S(1)} %copy-done, bf16[16,512]{1,0:T(8,128)(2,1)S(1)} %get-tuple-element.12, bf16[16,512]{1,0:T(8,128)(2,1)S(1)} %get-tuple-element.11), kind=kOutput, calls=%fused_computation.36 | convolution fusion | flops 67174400 | bytes 2392064 | tf_op jit(solution)/shard_map/cxy,jy->cxj/dot_general | solution.py:79
  15.1 0.0 all-reduce.2.cloned.1.call-update
  15.1 0.3 all-gather.2.cloned.1.call-start
  15.4 75.8 %reduce-scatter.2.cloned.1.call-done = f32[64,32,128]{2,1,0:T(8,128)} async-done(((f32[64,32,512]{2,1,0:T(8,128)}), f32[64,32,128]{2,1,0:T(8,128)}) %reduce-scatter.2.cloned.1.call-update) | async-done | bytes 1048592 | tf_op jit(solution)/shard_map/reduce_scatter | solution.py:82
  91.2 1.3 fusion.141
  92.5 0.0 copy-done.2
  92.5 0.0 copy-start.3
  92.5 0.6 fusion.45
  93.1 0.6 fusion.41
  93.7 0.6 fusion.36
  94.2 0.6 fusion.35
  94.9 1.1 copy.41
  96.0 0.0 copy-start.1
  96.0 0.0 all-gather.2.cloned.1.call-update
  96.0 0.1 multiply_convert_fusion.3
  96.1 0.1 multiply_convert_fusion.1
  96.3 0.0 copy-done.3
  96.3 4.8 %fusion.24 = f32[64,32,512]{2,0,1:T(8,128)} fusion(bf16[64,32,512]{2,1,0:T(8,128)(2,1)S(1)} %copy-done, bf16[64,64]{1,0:T(8,128)(2,1)S(1)} %copy-done.3), kind=kOutput, calls=%fused_computation.32 | convolution fusion | flops 134217728 | bytes 6299648 | tf_op jit(solution)/shard_map/cxy,co->oxy/dot_general | solution.py:102
  101.0 0.0 all-reduce.2.cloned.1.call-done
  101.0 1.1 fusion.142
  102.1 0.0 copy-done.1
  102.1 0.4 fusion.55
  102.5 0.4 fusion.53
  102.9 0.4 fusion.40
  103.3 0.4 fusion.39
  103.7 0.1 pad_maximum_fusion.1
  103.8 0.9 copy.57
  104.7 2.7 %fusion.77 = f32[64,32,512]{2,1,0:T(8,128)} fusion(bf16[64,32,32]{2,1,0:T(8,128)(2,1)S(1)} %copy.57, bf16[512,16]{0,1:T(8,128)(2,1)S(1)} %get-tuple-element.10, bf16[512,16]{0,1:T(8,128)(2,1)S(1)} %get-tuple-element.9), kind=kOutput, calls=%fused_computation.95 | convolution fusion | flops 67174400 | bytes 4358144 | tf_op jit(solution)/shard_map/oxj,yj->oxy/dot_general | solution.py:94
  107.3 35.6 %all-gather.2.cloned.1.call-done = bf16[64,32,512]{2,1,0:T(8,128)(2,1)} async-done(((bf16[64,32,128]{2,1,0:T(8,128)(2,1)}), bf16[64,32,512]{2,1,0:T(8,128)(2,1)}) %all-gather.2.cloned.1.call-update) | async-done | bytes 2097168 | tf_op jit(solution)/shard_map/all_gather | solution.py:86
  142.9 0.0 copy-start.4
  142.9 0.0 copy-start.5
  142.9 0.0 copy-start.6
  142.9 0.0 copy-start.7
  142.9 8.9 %fusion.19 = bf16[64,32,512]{2,1,0:T(8,128)(2,1)} fusion(f32[64,32,512]{2,0,1:T(8,128)} %fusion.24, f32[64,32,512]{2,1,0:T(8,128)} %fusion.77, bf16[64,32,512]{2,1,0:T(8,128)(2,1)} %all-gather.2.cloned.1.call-done, bf16[32,16]{0,1:T(8,128)(2,1)S(1)} %get-tuple-element.14, bf16[32,16]{0,1:T(8,128)(2,1)S(1)} %get-tuple-element.13), kind=kOutput, calls=%fused_computation.26 | convolution fusion | flops 72355840 | bytes 12584960 | tf_op jit(solution)/shard_map/ojy,xj->oxy/dot_general | solution.py:84
  151.9 0.0 copy-done.4
  151.9 0.0 copy-done.5
  151.9 0.0 copy-done.6
  151.9 0.0 copy-done.7
  151.9 57.8 %fusion.21 = bf16[64,32,512]{2,0,1:T(8,128)(2,1)} fusion(f32[64]{0:T(128)S(1)} %copy-done.7, f32[256]{0:T(256)S(1)} %copy-done.6, bf16[64,32,512]{2,1,0:T(8,128)(2,1)} %fusion.19, bf16[256,64]{0,1:T(8,128)(2,1)S(1)} %copy-done.4, bf16[64,256]{1,0:T(8,128)(2,1)S(1)} %copy-done.5), kind=kOutput, calls=%fused_computation.30 | convolution fusion | flops 1352663040 | bytes 4261120 | tf_op jit(solution)/shard_map/hxy,ho->oxy/dot_general | solution.py:110
  209.7 4.1 %copy.55 = bf16[64,32,512]{2,1,0:T(8,128)(2,1)} copy(bf16[64,32,512]{2,0,1:T(8,128)(2,1)} %fusion.21) | data formatting | bytes 4194304 | tf_op jit(solution)/shard_map/convert_element_type | solution.py:113
  (4 shorter events, 0.1 us)
Async XLA Ops:
  7.4 1.6 copy-start
  7.4 83.9 %reduce-scatter.2.cloned.1.call-start = ((), (), s32[]{:S(2)}) async-start(), calls=%async_computation.1 | async-start | bytes 5242880 | tf_op jit(solution)/shard_map/reduce_scatter | solution.py:82
  11.6 80.9 %copy-start.2 = (bf16[2,16,64,64]{3,2,1,0:T(8,128)(2,1)S(1)}, bf16[2,16,64,64]{3,2,1,0:T(8,128)(2,1)}, u32[]{:S(2)}) copy-start(bf16[2,16,64,64]{3,2,1,0:T(8,128)(2,1)} %param.9) | copy-start | bytes 786436
  11.6 89.4 %all-reduce.2.cloned.1.call-start = ((), (), s32[]{:S(2)}) async-start(), calls=%async_computation.3 | async-start | bytes 1048576 | tf_op jit(solution)/shard_map/psum | solution.py:92
  15.1 127.8 %all-gather.2.cloned.1.call-start = ((), (), s32[]{:S(2)}) async-start(), calls=%async_computation.2 | async-start | bytes 2621440 | tf_op jit(solution)/shard_map/all_gather | solution.py:86
  92.5 3.7 %copy-start.3 = (bf16[64,64]{1,0:T(8,128)(2,1)S(1)}, bf16[64,64]{1,0:T(8,128)(2,1)}, u32[]{:S(2)}) copy-start(bf16[64,64]{1,0:T(8,128)(2,1)} %param.11) | copy-start | bytes 24580
  96.0 6.1 %copy-start.1 = (bf16[2,16,64,64]{3,2,1,0:T(8,128)(2,1)S(1)}, bf16[2,16,64,64]{3,2,1,0:T(8,128)(2,1)}, u32[]{:S(2)}) copy-start(bf16[2,16,64,64]{3,2,1,0:T(8,128)(2,1)} %param.10) | copy-start | bytes 786436
  142.9 9.0 %copy-start.4 = (bf16[256,64]{0,1:T(8,128)(2,1)S(1)}, bf16[256,64]{0,1:T(8,128)(2,1)}, u32[]{:S(2)}) copy-start(bf16[256,64]{0,1:T(8,128)(2,1)} %param.14) | copy-start | bytes 98308
  142.9 9.0 %copy-start.5 = (bf16[64,256]{1,0:T(8,128)(2,1)S(1)}, bf16[64,256]{1,0:T(8,128)(2,1)}, u32[]{:S(2)}) copy-start(bf16[64,256]{1,0:T(8,128)(2,1)} %param.12) | copy-start | bytes 98308
  142.9 9.0 %copy-start.6 = (f32[256]{0:T(256)S(1)}, f32[256]{0:T(256)}, u32[]{:S(2)}) copy-start(f32[256]{0:T(256)} %param.13) | copy-start | bytes 3076
  142.9 9.0 %copy-start.7 = (f32[64]{0:T(128)S(1)}, f32[64]{0:T(128)}, u32[]{:S(2)}) copy-start(f32[64]{0:T(128)} %param.15) | copy-start | bytes 772
Sparse Core Ops, SparseCore 0:
  11.7 79.4 reduce-scatter.1
  96.1 46.7 all-gather.1
Sparse Core Ops, SparseCore 1:
  15.2 35.9 all-reduce.1
where the time goes:
time: 217 us; the launch traced here: 221 us
  waiting for transfers between devices  111 us (51%)
  matrix products  83.8 us (39%)
  between operations  15.2 us (7%)
  local copies, waits for them, and re-layouts  9.98 us (5%)
    reduce_scatter x1, waiting for transfers between devices, body(): lax.psum_scatter(row_partial, 'gx', scatter_dimension=2, tiled=True)  75.8 us
    dot_general x1, matrix products, body(): jnp.einsum('hxy,ho->oxy', hidden, down_weight, preferred_element_type=jnp...  57.8 us
    all_gather x1, waiting for transfers between devices, body(): lax.all_gather(mix_rows(row_share, row_weight), 'gx', axis=2, tiled=True)  35.6 us
    dot_general x1, matrix products, body(): jnp.einsum('ojy,xj->oxy', lax.all_gather(mix_rows(row_share, row_weight),...  8.95 us
    dot_general x1, matrix products, body(): jnp.einsum('cxy,co->oxy', plane_input, skip_weight, preferred_element_typ...  4.76 us
  transfers between devices with their start and end apart: 3, of which 2 were waited for; matrix products, arithmetic and copies ran while one was open for 9% of the time, Pallas kernels for 0%

commit v1 on v0

v1 whole, which is shorter than its diff:
```python
import math

import jax
import jax.numpy as jnp
import numpy as np
from jax import lax
from jax.experimental import pallas as pl
from jax.experimental.pallas import tpu as pltpu
from jax.sharding import PartitionSpec as P

LANES = 128
GROUP = 16
HALF_GROUP = 8
BIAS_ROWS = 16
TILE = 512
VMEM_BYTES = 48 * 1024 * 1024
HEAD_VMEM_BYTES = 63 * 1024 * 1024

TAIL = 0.4
COEFFS = (0.15957266, 0.16051476, 0.12055834, 0.14408696, -0.08478078)
EXP_SCALE = -0.5 * math.log2(math.e)


def gelu(v):
    t = jnp.abs(v)
    s = 1.0 / (1.0 + TAIL * t)
    poly = COEFFS[-1]
    for c in COEFFS[-2::-1]:
        poly = poly * s + c
    return jnp.maximum(v, 0.0) - jnp.exp2(t * t * EXP_SCALE) * (poly * s) * t


def row_tables(mode_count, shares, row_count):
    period = shares * row_count
    phases = np.arange(mode_count)[:, None] * np.arange(period)[None, :] % period
    angles = phases.astype(np.float64) * (2.0 * math.pi / period)
    table = np.stack([np.cos(angles), -np.sin(angles)], axis=1).reshape(2 * mode_count, shares, row_count)
    eye = np.eye(HALF_GROUP)
    whole = np.einsum("jsx,cd->sjcdx", table, eye)
    return jnp.asarray(
        whole.reshape(shares, 2 * mode_count * HALF_GROUP, HALF_GROUP * row_count), jnp.bfloat16
    )


def row_inverse_tables(mode_count, shares, row_count):
    period = shares * row_count
    phases = np.arange(period)[:, None] * np.arange(mode_count)[None, :] % period
    angles = phases.astype(np.float64) * (2.0 * math.pi / period)
    factors = np.where(np.arange(mode_count) == 0, 1.0, 2.0)
    table = np.stack([factors * np.cos(angles), -factors * np.sin(angles)], axis=2)
    table = table.reshape(shares, row_count, 2 * mode_count)
    whole = np.einsum("sxj,cd->sxcjd", table, np.eye(GROUP))
    return jnp.asarray(
        whole.reshape(shares, row_count * GROUP, 2 * mode_count * GROUP), jnp.bfloat16
    )


def forward_table(mode_count, period, offset, number):
    wave_index = jnp.arange(mode_count, dtype=jnp.int32)
    cell_index = offset + jnp.arange(number, dtype=jnp.int32)
    phases = wave_index[:, None] * cell_index[None, :] % period
    angles = phases.astype(jnp.float32) * (2.0 * math.pi / period)
    both = jnp.stack([jnp.cos(angles), -jnp.sin(angles)], axis=1)
    return both.reshape(2 * mode_count, number).astype(jnp.bfloat16)


def inverse_table(mode_count, period, offset, number):
    wave_index = jnp.arange(mode_count, dtype=jnp.int32)
    cell_index = offset + jnp.arange(number, dtype=jnp.int32)
    phases = wave_index[:, None] * cell_index[None, :] % period
    angles = phases.astype(jnp.float32) * (2.0 * math.pi / period)
    factors = jnp.where(wave_index == 0, 1.0, 2.0).astype(jnp.float32)[:, None]
    both = jnp.stack([factors * jnp.cos(angles), -factors * jnp.sin(angles)], axis=1)
    return both.reshape(2 * mode_count, number).astype(jnp.bfloat16)


def mix_kernel(row_ref, col_ref, row_out_ref, col_out_ref):
    for source, target in ((row_ref, row_out_ref), (col_ref, col_out_ref)):
        for k in range(source.shape[1]):
            real = source[0, k].astype(jnp.float32).T
            imag = source[1, k].astype(jnp.float32).T
            upper = jnp.concatenate([real, -imag], axis=1)
            lower = jnp.concatenate([imag, real], axis=1)
            target[k] = jnp.concatenate([upper, lower], axis=0).astype(jnp.bfloat16)


def mix_matrices(row_weight, col_weight):
    _, modes, channels, _ = row_weight.shape
    shape = jax.ShapeDtypeStruct((modes, 2 * channels, 2 * channels), jnp.bfloat16)
    return pl.pallas_call(
        mix_kernel,
        out_shape=(shape, shape),
        compiler_params=pltpu.CompilerParams(vmem_limit_bytes=VMEM_BYTES),
        cost_estimate=pl.CostEstimate(flops=10**8, bytes_accessed=2 * 2**20, transcendentals=0),
        name="mix_matrices",
    )(row_weight, col_weight)


def row_modes_kernel(place_ref, table_ref, send_in_ref, keep_in_ref, send_ref, keep_ref):
    table = table_ref[0]
    for source, target in ((send_in_ref, send_ref), (keep_in_ref, keep_ref)):
        parts = []
        for half in range(2):
            block = source[half * HALF_GROUP : (half + 1) * HALF_GROUP]
            block = block.reshape(-1, LANES)
            modes = jnp.dot(table, block, preferred_element_type=jnp.float32)
            parts.append(modes.reshape(-1, HALF_GROUP, LANES))
        target[...] = jnp.concatenate(parts, axis=1).astype(jnp.bfloat16)


def row_modes(place, tables, plane, mode_count):
    channels, row_count, _ = plane.shape
    shape = jax.ShapeDtypeStruct((2 * mode_count, channels, LANES), jnp.bfloat16)
    block = pl.BlockSpec((2 * mode_count, GROUP, LANES), lambda g, place: (0, g, 0))
    return pl.pallas_call(
        row_modes_kernel,
        out_shape=(shape, shape),
        grid_spec=pltpu.PrefetchScalarGridSpec(
            num_scalar_prefetch=1,
            grid=(channels // GROUP,),
            in_specs=[
                pl.BlockSpec((1,) + tables.shape[1:], lambda g, place: (place[2], 0, 0)),
                pl.BlockSpec((GROUP, row_count, LANES), lambda g, place: (g, 0, place[1])),
                pl.BlockSpec((GROUP, row_count, LANES), lambda g, place: (g, 0, place[0])),
            ],
            out_specs=(block, block),
        ),
        compiler_params=pltpu.CompilerParams(vmem_limit_bytes=HEAD_VMEM_BYTES),
        cost_estimate=pl.CostEstimate(flops=2 * 10**9, bytes_accessed=3 * 2**20, transcendentals=0),
        name="row_modes",
    )(place, tables, plane, plane)


def col_modes_kernel(table_ref, plane_ref, out_ref):
    block = plane_ref[...].reshape(-1, plane_ref.shape[2])
    out_ref[...] = lax.dot_general(
        table_ref[...], block, (((1,), (1,)), ((), ())), preferred_element_type=jnp.float32
    )


def col_modes(table, plane):
    channels, row_count, col_count = plane.shape
    modes = table.shape[0]
    return pl.pallas_call(
        col_modes_kernel,
        out_shape=jax.ShapeDtypeStruct((modes, channels * row_count), jnp.float32),
        grid=(channels // GROUP,),
        in_specs=[
            pl.BlockSpec((modes, col_count), lambda g: (0, 0)),
            pl.BlockSpec((GROUP, row_count, col_count), lambda g: (g, 0, 0)),
        ],
        out_specs=pl.BlockSpec((modes, GROUP * row_count), lambda g: (0, g)),
        compiler_params=pltpu.CompilerParams(vmem_limit_bytes=VMEM_BYTES),
        cost_estimate=pl.CostEstimate(flops=10**9, bytes_accessed=3 * 2**20, transcendentals=0),
        name="col_modes",
    )(table, plane)


def finish_kernel(
    row_scale,
    place_ref,
    modes_ref,
    mix_ref,
    inverse_ref,
    local_ref,
    plane_ref,
    col_ref,
    up_ref,
    down_ref,
    down_bias_ref,
    order_ref,
    *rest,
):
    out_ref, mixed_ref, pre_ref, done_ref, wide_ref = rest[-5:]
    mode_rows, channels, _ = modes_ref.shape
    row_count = plane_ref.shape[0]
    for k in range(mode_rows // 2):
        pair = modes_ref[2 * k : 2 * k + 2].reshape(2 * channels, LANES)
        mixed = jnp.dot(mix_ref[k], pair, preferred_element_type=jnp.float32) * row_scale
        mixed_ref[2 * k : 2 * k + 2] = mixed.astype(jnp.bfloat16).reshape(2, channels, LANES)
    for g in range(channels // GROUP):
        part = mixed_ref[:, g * GROUP : (g + 1) * GROUP, :].reshape(mode_rows * GROUP, LANES)
        rows = jnp.dot(inverse_ref[0], part, preferred_element_type=jnp.float32)
        pre_ref[:, g * GROUP : (g + 1) * GROUP, :] = rows.reshape(row_count, GROUP, LANES)
    cols = col_ref[...]

    def one_row(x):
        data = jnp.concatenate([plane_ref[x], cols], axis=0)
        local = jnp.dot(local_ref[x], data, preferred_element_type=jnp.float32)
        return (pre_ref[x] + local).astype(jnp.bfloat16)

    def gather(x, carry):
        at = pl.ds(pl.multiple_of(x * LANES, LANES), LANES)
        wide_ref[:channels, at] = one_row(x)
        return carry

    lax.fori_loop(0, row_count, gather, 0, unroll=32)
    wide_ref[channels:, :] = jnp.ones((BIAS_ROWS, wide_ref.shape[1]), jnp.bfloat16)
    bias = down_bias_ref[...]
    tiles = wide_ref.shape[1] // TILE

    def up(i):
        return jnp.dot(up_ref[...], wide_ref[:, i * TILE : (i + 1) * TILE], preferred_element_type=jnp.float32)

    def down(i, hidden):
        out = jnp.dot(down_ref[...], hidden, preferred_element_type=jnp.float32)
        for q in range(TILE // LANES):
            done_ref[i * (TILE // LANES) + q] = (out[:, q * LANES : (q + 1) * LANES] + bias).astype(jnp.bfloat16)

    waiting = up(0)
    hidden = None
    for i in range(tiles):
        following = up(i + 1) if i + 1 < tiles else None
        active = gelu(waiting).astype(jnp.bfloat16)
        if hidden is not None:
            down(i - 1, hidden)
        hidden, waiting = active, following
    down(tiles - 1, hidden)
    for g in range(channels // GROUP):
        for h in range(row_count // GROUP):
            o, x = slice(g * GROUP, (g + 1) * GROUP), slice(h * GROUP, (h + 1) * GROUP)
            block = done_ref[x, o, :].reshape(GROUP * GROUP, LANES)
            turned = jnp.dot(order_ref[...], block, preferred_element_type=jnp.float32)
            out_ref[o, x, :] = turned.astype(jnp.bfloat16).reshape(GROUP, GROUP, LANES)


def finish(place, which, modes, shared, plane_rows, col_inverse, row_scale, out):
    mix, inverse, local, up, down, down_bias, order = shared
    row_count, channels, col_count = plane_rows.shape

    def whole(a):
        return pl.BlockSpec(a.shape, lambda i, place: (0,) * a.ndim)

    operands = [modes, mix, inverse, local, plane_rows, col_inverse, up, down, down_bias, order]
    in_specs = [
        whole(modes),
        whole(mix),
        pl.BlockSpec((1,) + inverse.shape[1:], lambda i, place: (place[2], 0, 0)),
        whole(local),
        pl.BlockSpec((row_count, channels, LANES), lambda i, place: (0, 0, place[which])),
        pl.BlockSpec((col_inverse.shape[0], LANES), lambda i, place: (0, place[which])),
        whole(up),
        whole(down),
        whole(down_bias),
        whole(order),
    ]
    aliases = {}
    if out is not None:
        operands.append(out)
        in_specs.append(pl.BlockSpec(memory_space=pl.ANY))
        aliases = {len(operands): 0}

    def kernel(*refs):
        finish_kernel(row_scale, *refs)

    return pl.pallas_call(
        kernel,
        out_shape=jax.ShapeDtypeStruct((channels, row_count, col_count), jnp.bfloat16),
        grid_spec=pltpu.PrefetchScalarGridSpec(
            num_scalar_prefetch=1,
            grid=(1,),
            in_specs=in_specs,
            out_specs=pl.BlockSpec((channels, row_count, LANES), lambda i, place: (0, 0, place[which])),
            scratch_shapes=[
                pltpu.VMEM(modes.shape, jnp.bfloat16),
                pltpu.VMEM((row_count, channels, LANES), jnp.float32),
                pltpu.VMEM((row_count, channels, LANES), jnp.bfloat16),
                pltpu.VMEM((channels+BIAS_ROWS, row_count * LANES), jnp.bfloat16),
            ],
        ),
        input_output_aliases=aliases,
        compiler_params=pltpu.CompilerParams(vmem_limit_bytes=VMEM_BYTES),
        cost_estimate=pl.CostEstimate(flops=5 * 10**9, bytes_accessed=4 * 2**20, transcendentals=2 * 10**6),
        name="finish",
    )(place, *operands)


def add(a, b):
    return (a.astype(jnp.float32) + b.astype(jnp.float32)).astype(jnp.bfloat16)


NEAR = [(0, 1), (1, 0), (2, 3), (3, 2)]
FAR = [(0, 3), (3, 0), (1, 2), (2, 1)]


def sum_over_cols_axis(value):
    size = lax.axis_size("gy")
    if size & (size - 1):
        return lax.psum(value, "gy")
    step = 1
    while step < size:
        value = value + lax.ppermute(value, "gy", [(i, i ^ step) for i in range(size)])
        step *= 2
    return value


def body(
    plane_input, row_weight, col_weight, skip_weight, up_weight, up_bias, down_weight, down_bias
):
    channels, row_count, col_count = plane_input.shape
    mode_count = row_weight.shape[1]
    shares = lax.axis_size("gx")
    row_total = row_count * shares
    col_total = col_count * lax.axis_size("gy")
    row_scale = float(row_total * mode_count) ** (-0.5)
    col_scale = float(col_total * mode_count) ** (-0.5)
    share = lax.axis_index("gx")
    line = shares == 4
    inner = jnp.where((share == 1) | (share == 2), 1, 0) if line else jnp.zeros((), jnp.int32)
    rounds = col_count // (2 * LANES)
    places = [
        jnp.stack([2 * r + inner, 2 * r + 1 - inner, share]).astype(jnp.int32) for r in range(rounds)
    ]
    tables = row_tables(mode_count, shares, row_count)

    partial = [row_modes(places[r], tables, plane_input, mode_count) for r in range(rounds)]
    if line:
        near = [lax.ppermute(send, "gx", NEAR) for send, _ in partial]
        half = [add(keep, got) for (_, keep), got in zip(partial, near)]
        far = [lax.ppermute(value, "gx", FAR) for value in half]
        own = [add(value, got) for value, got in zip(half, far)]
        other = [lax.ppermute(value, "gx", NEAR) for value in own]
    else:
        own = [lax.psum(keep.astype(jnp.float32), "gx").astype(jnp.bfloat16) for _, keep in partial]
        other = [lax.psum(send.astype(jnp.float32), "gx").astype(jnp.bfloat16) for send, _ in partial]

    row_mix, col_mix = mix_matrices(row_weight, col_weight)
    col_offset = lax.axis_index("gy") * col_count
    col_partial = col_modes(forward_table(mode_count, col_total, col_offset, col_count), plane_input)
    col_spectrum = sum_over_cols_axis(col_partial)
    col_spectrum = col_spectrum.astype(jnp.bfloat16).reshape(mode_count, 2 * channels, row_count)
    col_mixed = jnp.einsum(
        "koc,kcx->kox", col_mix, col_spectrum, preferred_element_type=jnp.float32
    )
    col_mixed = (col_mixed * col_scale).astype(jnp.bfloat16)
    col_mixed = col_mixed.reshape(2 * mode_count, channels, row_count).transpose(2, 1, 0)
    skip = jnp.broadcast_to(skip_weight.T[None], (row_count, channels, channels))
    local = jnp.concatenate([skip, col_mixed], axis=2)
    col_inverse = inverse_table(mode_count, col_total, col_offset, col_count)
    high = lax.reduce_precision(up_bias, 8, 7)
    middle = lax.reduce_precision(up_bias - high, 8, 7)
    low = up_bias - high - middle
    bias_part = jnp.pad(jnp.stack([high, middle, low], axis=1), ((0, 0), (0, BIAS_ROWS - 3)))
    bias_part = bias_part.astype(jnp.bfloat16)
    up = jnp.concatenate([up_weight.T, bias_part], axis=1)
    order = np.zeros((GROUP, GROUP, GROUP, GROUP), np.float32)
    for a in range(GROUP):
        for b in range(GROUP):
            order[a, b, b, a] = 1.0
    order = jnp.asarray(order.reshape(GROUP * GROUP, GROUP * GROUP), jnp.bfloat16)
    shared = (
        row_mix,
        row_inverse_tables(mode_count, shares, row_count),
        local,
        up,
        down_weight.T,
        jnp.broadcast_to(down_bias[:, None], (channels, LANES)),
        order,
    )
    plane_rows = plane_input.transpose(1, 0, 2)
    out = None
    for r in range(rounds):
        for which, modes in ((0, own[r]), (1, other[r])):
            out = finish(places[r], which, modes, shared, plane_rows, col_inverse, row_scale, out)
    return out


def solution(mesh):
    placed = (P(None, ("grp", "gx"), "gy"), P(), P(), P(), P(), P(), P(), P())
    return jax.shard_map(
        body, mesh=mesh, in_specs=placed, out_specs=P(None, ("grp", "gx"), "gy"), check_vma=False
    )
```

time: 217 us -> 105 us (0.48); the launches traced: 221 us -> 104 us
  waiting for transfers between devices: 111 us -> 1.82 us
  matrix products: 83.8 us -> 1.45 us
  starting transfers between devices: 0.34 us -> 43.5 us
  Pallas kernels: 0 us -> 35.6 us
  between operations: 15.2 us -> 0.33 us
  other arithmetic: 0.55 us -> 11.5 us
    dot_general x14 -> x1, matrix products: 83.8 us -> 1.45 us  [body(): jnp.einsum('koc,kcx->kox', col_mix, col_spectrum, preferred_element_type=...]
    reduce_scatter x1 -> x0, waiting for transfers between devices: 75.8 us -> none  [body(): lax.psum_scatter(row_partial, 'gx', scatter_dimension=2, tiled=True)]
    ppermute x0 -> x8, starting transfers between devices: none -> 43.5 us  [the longest x2 31 us: body(): other = [lax.ppermute(value, 'gx', NEAR) for value in own]]
    pallas_call x0 -> x8, Pallas kernels: none -> 35.6 us  [the longest x4 24.2 us: finish(): pl.pallas_call(kernel, out_shape=jax.ShapeDtypeStruct((channels, row_coun...]
    all_gather x1 -> x0, waiting for transfers between devices: 35.6 us -> none  [body(): lax.all_gather(mix_rows(row_share, row_weight), 'gx', axis=2, tiled=True)]
    convert_element_type x0 -> x5, other arithmetic: none -> 6.1 us  [the longest x4 6.07 us: add(): return (a.astype(jnp.float32) + b.astype(jnp.float32)).astype(jnp.bfloat16)]
    unnamed x16 -> x36, local copies, waits for them, and re-layouts: 1.55 us -> 6.04 us
    convert_element_type x1 -> x3, local copies, waits for them, and re-layouts: 4.07 us -> 0.11 us  [the longest x1 0.07 us: body(): col_mixed = (col_mixed * col_scale).astype(jnp.bfloat16)]
  transfers between devices with their start and end apart: 3 -> 8, of which waited for: 2 -> 1; matrix products, arithmetic and copies ran while one was open for 9% -> 19% of each run, Pallas kernels for 0% -> 24%
where the time goes in v1:
time: 105 us; the launch traced here: 104 us
  starting transfers between devices  43.5 us (41%)
  Pallas kernels  35.6 us (34%)
  other arithmetic  11.5 us (11%)
  local copies, waits for them, and re-layouts  9.68 us (9%)
  waiting for transfers between devices  1.82 us (2%)
  matrix products  1.45 us (1%)
    ppermute x2, starting transfers between devices, body(): other = [lax.ppermute(value, 'gx', NEAR) for value in own]  31 us
    pallas_call x4, Pallas kernels, finish(): pl.pallas_call(kernel, out_shape=jax.ShapeDtypeStruct((channels, row_coun...  24.2 us
    pallas_call x2, Pallas kernels, row_modes(): pl.pallas_call(row_modes_kernel, out_shape=(shape, shape), grid_spec=pltp...  9.61 us
    ppermute x2, starting transfers between devices, body(): far = [lax.ppermute(value, 'gx', FAR) for value in half]  7.42 us
    convert_element_type x4, other arithmetic, add(): return (a.astype(jnp.float32) + b.astype(jnp.float32)).astype(jnp.bfloat16)  6.07 us
    unnamed x36, local copies, waits for them, and re-layouts  6.04 us
    ppermute x2, starting transfers between devices, body(): near = [lax.ppermute(send, 'gx', NEAR) for send, _ in partial]  3.05 us
  transfers between devices with their start and end apart: 8, of which 1 were waited for; matrix products, arithmetic and copies ran while one was open for 19% of the time, Pallas kernels for 24%

profile of v1, /device:TPU:0, one launch (start us, length us, event | category | flops | bytes accessed | tf_op | source)
XLA Modules:
  0.0 104.0 jit_solution(8898904967372387484)
XLA Ops:
  0.0 0.6 add_add_fusion.1.place_ref.refs_0_
  0.6 4.8 %row_modes.3 = (bf16[32,64,128]{2,1,0:T(8,128)(2,1)}, bf16[32,64,128]{2,1,0:T(8,128)(2,1)}) custom-call(s32[3]{0:T(128)} %add_add_fusion.1.place_ref.refs_0_, bf16[4,256,256]{2,1,0:T(8,128)(2,1)} %constant.52.clone.table_ref, bf16[64,32,512]{2,1,0:T(8,128)(2,1)} %keep_in_ref.3, bf16[64,32,512]{2,1,0:T(8,128)(2,1)} %keep_in_ref.3), custom_call_target="tpu_custom_call" | custom-call | flops 2000000000 | bytes 3145728 | tf_op jit(solution)/shard_map/row_modes/pallas_call | solution.py:115
  5.4 3.0 %collective-permute-start.5 = (bf16[32,64,128]{2,1,0:T(8,128)(2,1)}, bf16[32,64,128]{2,1,0:T(8,128)(2,1)}, u32[]{:S(2)}, u32[]{:S(2)}) collective-permute-start(bf16[32,64,128]{2,1,0:T(8,128)(2,1)} %get-tuple-element.16), channel_id=1, source_target_pairs={{0,4},{4,0},{8,12},{12,8},{1,5},{5,1},{9,13},{13,9},{2,6},{6,2},{1... | collective-permute-start | bytes 1572872 | tf_op jit(solution)/shard_map/ppermute | solution.py:318
  8.4 0.2 multiply_convert_fusion.1
  8.6 0.0 copy-start
  8.7 1.6 %copy-done = bf16[64,32,512]{2,1,0:T(8,128)(2,1)S(1)} copy-done((bf16[64,32,512]{2,1,0:T(8,128)(2,1)S(1)}, bf16[64,32,512]{2,1,0:T(8,128)(2,1)}, u32[]{:S(2)}) %copy-start) | copy-done | bytes 2097176
  10.2 1.1 %col_modes.1 = f32[32,2048]{1,0:T(8,128)S(1)} custom-call(bf16[32,512]{1,0:T(8,128)(2,1)S(1)} %convert_element_type.81.table_ref, bf16[64,32,512]{2,1,0:T(8,128)(2,1)S(1)} %copy-done), custom_call_target="tpu_custom_call" | custom-call | flops 1000000000 | bytes 3145728 | tf_op jit(solution)/shard_map/col_modes/pallas_call | solution.py:144
  11.3 0.1 collective-permute-start.3
  11.4 0.6 add_add_fusion.place_ref.refs_0_
  12.0 4.9 %row_modes.2 = (bf16[32,64,128]{2,1,0:T(8,128)(2,1)}, bf16[32,64,128]{2,1,0:T(8,128)(2,1)}) custom-call(s32[3]{0:T(128)} %add_add_fusion.place_ref.refs_0_, bf16[4,256,256]{2,1,0:T(8,128)(2,1)} %constant.52.clone.table_ref, bf16[64,32,512]{2,1,0:T(8,128)(2,1)} %keep_in_ref.3, bf16[64,32,512]{2,1,0:T(8,128)(2,1)} %keep_in_ref.3), custom_call_target="tpu_custom_call" | custom-call | flops 2000000000 | bytes 3145728 | tf_op jit(solution)/shard_map/row_modes/pallas_call | solution.py:115
  16.9 0.0 collective-permute-start
  16.9 0.0 copy-done.15
  16.9 0.0 copy-start.13
  17.0 0.0 copy-start.1
  17.0 0.0 copy-start.2
  17.0 2.8 %copy.46 = bf16[64,32,512]{2,0,1:T(8,128)(2,1)S(1)} copy(bf16[64,32,512]{2,1,0:T(8,128)(2,1)} %keep_in_ref.3) | data formatting | bytes 4194304 | tf_op args[0]
  19.8 0.0 copy-done.14
  19.8 0.1 copy.35
  20.0 0.6 pad_maximum_fusion.3
  20.6 0.8 copy.43
  21.4 0.0 copy-done.13
  21.4 0.7 copy.42
  22.2 0.0 copy-done.1
  22.2 0.0 copy-done.2
  22.2 0.7 mix_matrices.1
  22.9 0.8 copy-done.3
  23.7 1.0 fusion.2.refs_7_
  24.7 0.0 collective-permute-done.3
  24.7 1.0 add.68
  25.7 2.0 %collective-permute-start.4 = (f32[32,2048]{1,0:T(8,128)S(1)}, f32[32,2048]{1,0:T(8,128)S(1)}, u32[]{:S(2)}, u32[]{:S(2)}) collective-permute-start(f32[32,2048]{1,0:T(8,128)S(1)} %add.68), channel_id=1, source_target_pairs={{0,2},{1,3},{2,0},{3,1},{4,6},{5,7},{6,4},{7,5},{8,10},{9,11},{10,... | collective-permute-start | bytes 786440 | tf_op jit(solution)/shard_map/ppermute | solution.py:292
  27.6 0.0 collective-permute-done.5
  27.7 1.3 %add_convert_fusion.1 = bf16[32,64,128]{2,1,0:T(8,128)(2,1)S(1)} fusion(bf16[32,64,128]{2,1,0:T(8,128)(2,1)} %collective-permute-done.5, bf16[32,64,128]{2,1,0:T(8,128)(2,1)S(1)} %copy-done.12), kind=kLoop, calls=%fused_computation.4 | loop fusion | flops 1048576 | bytes 1572864 | tf_op jit(solution)/shard_map/convert_element_type | solution.py:279
  28.9 3.7 %collective-permute-start.6 = (bf16[32,64,128]{2,1,0:T(8,128)(2,1)S(1)}, bf16[32,64,128]{2,1,0:T(8,128)(2,1)}, u32[]{:S(2)}, u32[]{:S(2)}) collective-permute-start(bf16[32,64,128]{2,1,0:T(8,128)(2,1)S(1)} %add_convert_fusion.1), channel_id=1, source_target_pairs={{0,12},{12,0},{4,8},{8,4},{1,13},{13,1},{5,9},{9,5},{2,14},{14,2},... | collective-permute-start | bytes 1572872 | tf_op jit(solution)/shard_map/ppermute | solution.py:320
  32.6 1.8 %collective-permute-done.4 = f32[32,2048]{1,0:T(8,128)S(1)} collective-permute-done((f32[32,2048]{1,0:T(8,128)S(1)}, f32[32,2048]{1,0:T(8,128)S(1)}, u32[]{:S(2)}, u32[]{:S(2)}) %collective-permute-start.4) | collective-permute-done | bytes 262176 | tf_op jit(solution)/shard_map/ppermute | solution.py:292
  34.5 1.2 %reshape.205 = bf16[16,128,32]{2,1,0:T(8,128)(2,1)} reshape(bf16[32,2048]{1,0:T(8,128)(2,1)S(1)} %add_convert_fusion.4) | data formatting | bytes 262144 | tf_op jit(solution)/shard_map/reshape | solution.py:331
  35.6 0.0 collective-permute-done
  35.6 2.2 %add_convert_fusion.3 = bf16[32,64,128]{2,1,0:T(8,128)(2,1)} fusion(bf16[32,64,128]{2,1,0:T(8,128)(2,1)} %collective-permute-done, bf16[32,64,128]{2,1,0:T(8,128)(2,1)} %get-tuple-element.11), kind=kLoop, calls=%fused_computation.6 | loop fusion | flops 1048576 | bytes 1572864 | tf_op jit(solution)/shard_map/convert_element_type | solution.py:279
  37.8 3.8 %collective-permute-start.1 = (bf16[32,64,128]{2,1,0:T(8,128)(2,1)}, bf16[32,64,128]{2,1,0:T(8,128)(2,1)}, u32[]{:S(2)}, u32[]{:S(2)}) collective-permute-start(bf16[32,64,128]{2,1,0:T(8,128)(2,1)} %add_convert_fusion.3), channel_id=1, source_target_pairs={{0,12},{12,0},{4,8},{8,4},{1,13},{13,1},{5,9},{9,5},{2,14},{14,2},... | collective-permute-start | bytes 1572872 | tf_op jit(solution)/shard_map/ppermute | solution.py:320
  41.6 1.5 %fusion = bf16[16,128,32]{1,2,0:T(8,128)(2,1)S(1)} fusion(bf16[16,128,128]{2,1,0:T(8,128)(2,1)S(1)} %copy-done.4, bf16[16,128,32]{2,1,0:T(8,128)(2,1)} %reshape.205), kind=kOutput, calls=%fused_computation.2 | convolution fusion | flops 16908288 | bytes 786432 | tf_op jit(solution)/shard_map/koc,kcx->kox/dot_general | solution.py:332
  43.0 0.1 copy.38
  43.1 0.1 reshape.206
  43.2 1.0 %copy.39 = bf16[32,64,32]{0,1,2:T(8,128)(2,1)} copy(bf16[32,64,32]{1,0,2:T(8,128)(2,1)S(1)} %reshape.206) | data formatting | bytes 262144 | tf_op jit(solution)/shard_map/reshape | solution.py:336
  44.3 0.1 broadcast_in_dim.12
  44.4 0.0 copy-start.16
  44.4 0.0 copy-start.5
  44.4 0.0 copy-start.8
  44.4 0.0 copy-start.9
  44.5 0.0 copy-start.10
  44.5 0.0 copy-start.11
  44.5 1.5 %pad_maximum_fusion.refs_4_ = bf16[32,64,96]{2,1,0:T(8,128)(2,1)S(1)} fusion(bf16[32,64,32]{2,1,0:T(8,128)(2,1)} %bitcast.24, bf16[32,64,64]{2,1,0:T(8,128)(2,1)S(1)} %broadcast_in_dim.12), kind=kLoop, calls=%fused_computation.7 | loop fusion | flops 786432 | bytes 786432 | tf_op jit(solution)/shard_map/concatenate | solution.py:338
  46.0 0.0 collective-permute-done.6
  46.0 1.2 %add_convert_fusion.refs_1_ = bf16[32,64,128]{2,1,0:T(8,128)(2,1)S(1)} fusion(bf16[32,64,128]{2,1,0:T(8,128)(2,1)} %collective-permute-done.6, bf16[32,64,128]{2,1,0:T(8,128)(2,1)S(1)} %add_convert_fusion.1), kind=kLoop, calls=%fused_computation.3 | loop fusion | flops 1048576 | bytes 1572864 | tf_op jit(solution)/shard_map/convert_element_type | solution.py:279
  47.2 22.0 %collective-permute-start.7 = (bf16[32,64,128]{2,1,0:T(8,128)(2,1)S(1)}, bf16[32,64,128]{2,1,0:T(8,128)(2,1)S(1)}, u32[]{:S(2)}, u32[]{:S(2)}) collective-permute-start(bf16[32,64,128]{2,1,0:T(8,128)(2,1)S(1)} %add_convert_fusion.refs_1_), channel_id=1, source_target_pairs={{0,4},{4,0},{8,12},{12,8},{1,5},{5,1},{9,13},{13,9},{2,6},{6,2},{1... | collective-permute-start | bytes 1572872 | tf_op jit(solution)/shard_map/ppermute | solution.py:322
  69.2 0.0 collective-permute-done.1
  69.2 1.4 %add_convert_fusion.2.refs_1_ = bf16[32,64,128]{2,1,0:T(8,128)(2,1)S(1)} fusion(bf16[32,64,128]{2,1,0:T(8,128)(2,1)} %collective-permute-done.1, bf16[32,64,128]{2,1,0:T(8,128)(2,1)} %add_convert_fusion.3), kind=kLoop, calls=%fused_computation.5 | loop fusion | flops 1048576 | bytes 1572864 | tf_op jit(solution)/shard_map/convert_element_type | solution.py:279
  70.6 9.0 %collective-permute-start.2 = (bf16[32,64,128]{2,1,0:T(8,128)(2,1)S(1)}, bf16[32,64,128]{2,1,0:T(8,128)(2,1)S(1)}, u32[]{:S(2)}, u32[]{:S(2)}) collective-permute-start(bf16[32,64,128]{2,1,0:T(8,128)(2,1)S(1)} %add_convert_fusion.2.refs_1_), channel_id=1, source_target_pairs={{0,4},{4,0},{8,12},{12,8},{1,5},{5,1},{9,13},{13,9},{2,6},{6,2},{1... | collective-permute-start | bytes 1572872 | tf_op jit(solution)/shard_map/ppermute | solution.py:322
  79.6 0.1 broadcast_in_dim.15.refs_9_
  79.7 0.0 copy-done.8
  79.7 6.0 %finish.4.refs_11_ = bf16[64,32,512]{2,1,0:T(8,128)(2,1)} custom-call(s32[3]{0:T(128)S(1)} %copy-done.5, bf16[32,64,128]{2,1,0:T(8,128)(2,1)S(1)} %add_convert_fusion.refs_1_, bf16[16,128,128]{2,1,0:T(8,128)(2,1)S(1)} %copy-done.8, bf16[4,512,512]{2,1,0:T(8,128)(2,1)S(1)} %copy-done.10, bf16[32,64,96]{2,1,0:T(8,128)(2,1)S(1)} %pad_maximum_fusion.refs_4_, ...), custom_call_target="tpu_custom_call" | custom-call | flops 5000000000 | bytes 4194304 | tf_op jit(solution)/shard_map/finish/pallas_call | solution.py:256
  85.7 0.0 collective-permute-done.7.refs_1_
  85.7 6.2 %finish.5.refs_11_ = bf16[64,32,512]{2,1,0:T(8,128)(2,1)} custom-call(s32[3]{0:T(128)S(1)} %copy-done.5, bf16[32,64,128]{2,1,0:T(8,128)(2,1)S(1)} %collective-permute-done.7.refs_1_, bf16[16,128,128]{2,1,0:T(8,128)(2,1)S(1)} %copy-done.8, bf16[4,512,512]{2,1,0:T(8,128)(2,1)S(1)} %copy-done.10, ...), custom_call_target="tpu_custom_call", output_to_operand_aliasing={{}: (11, {})} | custom-call | flops 5000000000 | bytes 4194304 | tf_op jit(solution)/shard_map/finish/pallas_call | solution.py:256
  91.9 6.0 %finish.6.refs_11_ = bf16[64,32,512]{2,1,0:T(8,128)(2,1)} custom-call(s32[3]{0:T(128)S(1)} %copy-done.6, bf16[32,64,128]{2,1,0:T(8,128)(2,1)S(1)} %add_convert_fusion.2.refs_1_, bf16[16,128,128]{2,1,0:T(8,128)(2,1)S(1)} %copy-done.8, bf16[4,512,512]{2,1,0:T(8,128)(2,1)S(1)} %copy-done.10, ...), custom_call_target="tpu_custom_call", output_to_operand_aliasing={{}: (11, {})} | custom-call | flops 5000000000 | bytes 4194304 | tf_op jit(solution)/shard_map/finish/pallas_call | solution.py:256
  97.9 0.0 collective-permute-done.2.refs_1_
  97.9 6.0 %finish.7 = bf16[64,32,512]{2,1,0:T(8,128)(2,1)} custom-call(s32[3]{0:T(128)S(1)} %copy-done.6, bf16[32,64,128]{2,1,0:T(8,128)(2,1)S(1)} %collective-permute-done.2.refs_1_, bf16[16,128,128]{2,1,0:T(8,128)(2,1)S(1)} %copy-done.8, bf16[4,512,512]{2,1,0:T(8,128)(2,1)S(1)} %copy-done.10, ...), custom_call_target="tpu_custom_call", output_to_operand_aliasing={{}: (11, {})} | custom-call | flops 5000000000 | bytes 4194304 | tf_op jit(solution)/shard_map/finish/pallas_call | solution.py:256
  (29 shorter events, 0.2 us)
Async XLA Ops:
  5.4 22.3 %collective-permute-start.5 = (bf16[32,64,128]{2,1,0:T(8,128)(2,1)}, bf16[32,64,128]{2,1,0:T(8,128)(2,1)}, u32[]{:S(2)}, u32[]{:S(2)}) collective-permute-start(bf16[32,64,128]{2,1,0:T(8,128)(2,1)} %get-tuple-element.16), channel_id=1, source_target_pairs={{0,4},{4,0},{8,12},{12,8},{1,5},{5,1},{9,13},{13,9},{2,6},{6,2},{1... | collective-permute-start | bytes 1572872 | tf_op jit(solution)/shard_map/ppermute | solution.py:318
  8.6 1.6 %copy-start = (bf16[64,32,512]{2,1,0:T(8,128)(2,1)S(1)}, bf16[64,32,512]{2,1,0:T(8,128)(2,1)}, u32[]{:S(2)}) copy-start(bf16[64,32,512]{2,1,0:T(8,128)(2,1)} %keep_in_ref.3) | copy-start | bytes 6291460
  11.3 13.3 %collective-permute-start.3 = (f32[32,2048]{1,0:T(8,128)S(1)}, f32[32,2048]{1,0:T(8,128)}, u32[]{:S(2)}, u32[]{:S(2)}) collective-permute-start(f32[32,2048]{1,0:T(8,128)S(1)} %col_modes.1), channel_id=1, source_target_pairs={{0,1},{1,0},{2,3},{3,2},{4,5},{5,4},{6,7},{7,6},{8,9},{9,8},{10,11... | collective-permute-start | bytes 786440 | tf_op jit(solution)/shard_map/ppermute | solution.py:292
  12.0 4.9 %copy-start.15 = (f32[256]{0:T(256)S(1)}, f32[256]{0:T(256)}, u32[]{:S(2)}) copy-start(f32[256]{0:T(256)} %param.16) | copy-start | bytes 3076
  16.9 18.7 %collective-permute-start = (bf16[32,64,128]{2,1,0:T(8,128)(2,1)}, bf16[32,64,128]{2,1,0:T(8,128)(2,1)}, u32[]{:S(2)}, u32[]{:S(2)}) collective-permute-start(bf16[32,64,128]{2,1,0:T(8,128)(2,1)} %get-tuple-element.12), channel_id=1, source_target_pairs={{0,4},{4,0},{8,12},{12,8},{1,5},{5,1},{9,13},{13,9},{2,6},{6,2},{1... | collective-permute-start | bytes 1572872 | tf_op jit(solution)/shard_map/ppermute | solution.py:318
  16.9 2.9 %copy-start.14 = (bf16[64,64]{1,0:T(8,128)(2,1)S(1)}, bf16[64,64]{1,0:T(8,128)(2,1)}, u32[]{:S(2)}) copy-start(bf16[64,64]{1,0:T(8,128)(2,1)} %param.14) | copy-start | bytes 24580
  16.9 4.5 %copy-start.13 = (bf16[64,256]{1,0:T(8,128)(2,1)S(1)}, bf16[64,256]{1,0:T(8,128)(2,1)}, u32[]{:S(2)}) copy-start(bf16[64,256]{1,0:T(8,128)(2,1)} %param.15) | copy-start | bytes 98308
  17.0 5.2 %copy-start.1 = (bf16[2,16,64,64]{3,2,1,0:T(8,128)(2,1)S(1)}, bf16[2,16,64,64]{3,2,1,0:T(8,128)(2,1)}, u32[]{:S(2)}) copy-start(bf16[2,16,64,64]{3,2,1,0:T(8,128)(2,1)} %row_ref.1) | copy-start | bytes 786436
  17.0 5.2 %copy-start.2 = (bf16[2,16,64,64]{3,2,1,0:T(8,128)(2,1)S(1)}, bf16[2,16,64,64]{3,2,1,0:T(8,128)(2,1)}, u32[]{:S(2)}) copy-start(bf16[2,16,64,64]{3,2,1,0:T(8,128)(2,1)} %col_ref.1) | copy-start | bytes 786436
  22.2 5.5 %copy-start.12 = (bf16[32,64,128]{2,1,0:T(8,128)(2,1)S(1)}, bf16[32,64,128]{2,1,0:T(8,128)(2,1)}, u32[]{:S(2)}) copy-start(bf16[32,64,128]{2,1,0:T(8,128)(2,1)} %get-tuple-element.15) | copy-start | bytes 1572868
  22.9 0.8 copy-start.3
  23.7 4.0 %copy-start.7 = (bf16[16,128,128]{2,1,0:T(8,128)(2,1)}, bf16[16,128,128]{2,1,0:T(8,128)(2,1)S(1)}, u32[]{:S(2)}) copy-start(bf16[16,128,128]{2,1,0:T(8,128)(2,1)S(1)} %get-tuple-element.13.refs_2_) | copy-start | bytes 1572868
  25.7 8.8 %collective-permute-start.4 = (f32[32,2048]{1,0:T(8,128)S(1)}, f32[32,2048]{1,0:T(8,128)S(1)}, u32[]{:S(2)}, u32[]{:S(2)}) collective-permute-start(f32[32,2048]{1,0:T(8,128)S(1)} %add.68), channel_id=1, source_target_pairs={{0,2},{1,3},{2,0},{3,1},{4,6},{5,7},{6,4},{7,5},{8,10},{9,11},{10,... | collective-permute-start | bytes 786440 | tf_op jit(solution)/shard_map/ppermute | solution.py:292
  27.6 13.9 %copy-start.4 = (bf16[16,128,128]{2,1,0:T(8,128)(2,1)S(1)}, bf16[16,128,128]{2,1,0:T(8,128)(2,1)}, u32[]{:S(2)}) copy-start(bf16[16,128,128]{2,1,0:T(8,128)(2,1)} %copy-done.3) | copy-start | bytes 1572868
  28.9 17.0 %collective-permute-start.6 = (bf16[32,64,128]{2,1,0:T(8,128)(2,1)S(1)}, bf16[32,64,128]{2,1,0:T(8,128)(2,1)}, u32[]{:S(2)}, u32[]{:S(2)}) collective-permute-start(bf16[32,64,128]{2,1,0:T(8,128)(2,1)S(1)} %add_convert_fusion.1), channel_id=1, source_target_pairs={{0,12},{12,0},{4,8},{8,4},{1,13},{13,1},{5,9},{9,5},{2,14},{14,2},... | collective-permute-start | bytes 1572872 | tf_op jit(solution)/shard_map/ppermute | solution.py:320
  37.8 31.4 %collective-permute-start.1 = (bf16[32,64,128]{2,1,0:T(8,128)(2,1)}, bf16[32,64,128]{2,1,0:T(8,128)(2,1)}, u32[]{:S(2)}, u32[]{:S(2)}) collective-permute-start(bf16[32,64,128]{2,1,0:T(8,128)(2,1)} %add_convert_fusion.3), channel_id=1, source_target_pairs={{0,12},{12,0},{4,8},{8,4},{1,13},{13,1},{5,9},{9,5},{2,14},{14,2},... | collective-permute-start | bytes 1572872 | tf_op jit(solution)/shard_map/ppermute | solution.py:320
  44.4 35.2 %copy-start.16 = (f32[64]{0:T(128)S(1)}, f32[64]{0:T(128)}, u32[]{:S(2)}) copy-start(f32[64]{0:T(128)} %param.18) | copy-start | bytes 772
  44.4 35.3 %copy-start.5 = (s32[3]{0:T(128)S(1)}, s32[3]{0:T(128)}, u32[]{:S(2)}) copy-start(s32[3]{0:T(128)} %add_add_fusion.1.place_ref.refs_0_) | copy-start | bytes 40
  44.4 35.3 %copy-start.8 = (bf16[16,128,128]{2,1,0:T(8,128)(2,1)S(1)}, bf16[16,128,128]{2,1,0:T(8,128)(2,1)}, u32[]{:S(2)}) copy-start(bf16[16,128,128]{2,1,0:T(8,128)(2,1)} %copy-done.7) | copy-start | bytes 1572868
  44.4 35.3 %copy-start.9 = (bf16[256,64]{0,1:T(8,128)(2,1)S(1)}, bf16[256,64]{0,1:T(8,128)(2,1)}, u32[]{:S(2)}) copy-start(bf16[256,64]{0,1:T(8,128)(2,1)} %param.17) | copy-start | bytes 98308
  44.5 35.2 %copy-start.10 = (bf16[4,512,512]{2,1,0:T(8,128)(2,1)S(1)}, bf16[4,512,512]{2,1,0:T(8,128)(2,1)}, u32[]{:S(2)}) copy-start(bf16[4,512,512]{2,1,0:T(8,128)(2,1)} %constant.54.clone.refs_3_) | copy-start | bytes 6291460
  44.5 35.2 %copy-start.11 = (bf16[256,256]{1,0:T(8,128)(2,1)S(1)}, bf16[256,256]{1,0:T(8,128)(2,1)}, u32[]{:S(2)}) copy-start(bf16[256,256]{1,0:T(8,128)(2,1)} %constant.53.clone.refs_10_) | copy-start | bytes 393220
  47.2 38.5 %collective-permute-start.7 = (bf16[32,64,128]{2,1,0:T(8,128)(2,1)S(1)}, bf16[32,64,128]{2,1,0:T(8,128)(2,1)S(1)}, u32[]{:S(2)}, u32[]{:S(2)}) collective-permute-start(bf16[32,64,128]{2,1,0:T(8,128)(2,1)S(1)} %add_convert_fusion.refs_1_), channel_id=1, source_target_pairs={{0,4},{4,0},{8,12},{12,8},{1,5},{5,1},{9,13},{13,9},{2,6},{6,2},{1... | collective-permute-start | bytes 1572872 | tf_op jit(solution)/shard_map/ppermute | solution.py:322
  70.6 27.3 %collective-permute-start.2 = (bf16[32,64,128]{2,1,0:T(8,128)(2,1)S(1)}, bf16[32,64,128]{2,1,0:T(8,128)(2,1)S(1)}, u32[]{:S(2)}, u32[]{:S(2)}) collective-permute-start(bf16[32,64,128]{2,1,0:T(8,128)(2,1)S(1)} %add_convert_fusion.2.refs_1_), channel_id=1, source_target_pairs={{0,4},{4,0},{8,12},{12,8},{1,5},{5,1},{9,13},{13,9},{2,6},{6,2},{1... | collective-permute-start | bytes 1572872 | tf_op jit(solution)/shard_map/ppermute | solution.py:322
  85.7 6.2 %copy-start.6 = (s32[3]{0:T(128)S(1)}, s32[3]{0:T(128)}, u32[]{:S(2)}) copy-start(s32[3]{0:T(128)} %add_add_fusion.place_ref.refs_0_) | copy-start | bytes 40

commit v2 on v1

--- a/solution.py
+++ b/solution.py
@@ -12,8 +12,9 @@
 GROUP = 16
 HALF_GROUP = 8
 BIAS_ROWS = 16
+STEP_CHANNELS = 32
 TILE = 512
-VMEM_BYTES = 48 * 1024 * 1024
+VMEM_BYTES = 24 * 1024 * 1024
 HEAD_VMEM_BYTES = 63 * 1024 * 1024
 
 TAIL = 0.4
@@ -91,44 +92,57 @@
         mix_kernel,
         out_shape=(shape, shape),
         compiler_params=pltpu.CompilerParams(vmem_limit_bytes=VMEM_BYTES),
-        cost_estimate=pl.CostEstimate(flops=10**8, bytes_accessed=2 * 2**20, transcendentals=0),
+        cost_estimate=pl.CostEstimate(flops=0, bytes_accessed=0, transcendentals=0),
         name="mix_matrices",
     )(row_weight, col_weight)
 
 
-def row_modes_kernel(place_ref, table_ref, send_in_ref, keep_in_ref, send_ref, keep_ref):
-    table = table_ref[0]
-    for source, target in ((send_in_ref, send_ref), (keep_in_ref, keep_ref)):
-        parts = []
-        for half in range(2):
-            block = source[half * HALF_GROUP : (half + 1) * HALF_GROUP]
-            block = block.reshape(-1, LANES)
-            modes = jnp.dot(table, block, preferred_element_type=jnp.float32)
-            parts.append(modes.reshape(-1, HALF_GROUP, LANES))
-        target[...] = jnp.concatenate(parts, axis=1).astype(jnp.bfloat16)
-
-
-def row_modes(place, tables, plane, mode_count):
+def row_modes_kernel(place_ref, *refs):
+    for table, source, target in zip(refs[0:2], refs[2:4], refs[4:6]):
+        for g in range(source.shape[0] // GROUP):
+            parts = []
+            for half in range(2):
+                first = g * GROUP + half * HALF_GROUP
+                block = source[first : first + HALF_GROUP].reshape(-1, LANES)
+                modes = jnp.dot(table[0], block, preferred_element_type=jnp.float32)
+                parts.append(modes.reshape(-1, HALF_GROUP, LANES))
+            at = slice(g * GROUP, (g + 1) * GROUP)
+            target[:, at, :] = jnp.concatenate(parts, axis=1).astype(jnp.bfloat16)
+
+
+def row_modes(place, tables, plane, mode_count, base, paired):
     channels, row_count, _ = plane.shape
-    shape = jax.ShapeDtypeStruct((2 * mode_count, channels, LANES), jnp.bfloat16)
-    block = pl.BlockSpec((2 * mode_count, GROUP, LANES), lambda g, place: (0, g, 0))
+    modes = 2 * mode_count if paired else mode_count
+    groups = channels // STEP_CHANNELS
+    shape = jax.ShapeDtypeStruct((modes, channels, LANES), jnp.bfloat16)
+    block = pl.BlockSpec((modes, STEP_CHANNELS, LANES), lambda g, place: (0, g, 0))
+    rows = modes * HALF_GROUP
+
+    def table_at(which):
+        return pl.BlockSpec(
+            (1, rows, tables.shape[2]),
+            lambda g, place: (place[2], 0 if paired else place[which], 0),
+        )
+
+    def plane_at(which):
+        return pl.BlockSpec(
+            (STEP_CHANNELS, row_count, LANES),
+            lambda g, place: (g, 0, base + place[which] if paired else base),
+        )
+
     return pl.pallas_call(
         row_modes_kernel,
         out_shape=(shape, shape),
         grid_spec=pltpu.PrefetchScalarGridSpec(
             num_scalar_prefetch=1,
-            grid=(channels // GROUP,),
-            in_specs=[
-                pl.BlockSpec((1,) + tables.shape[1:], lambda g, place: (place[2], 0, 0)),
-                pl.BlockSpec((GROUP, row_count, LANES), lambda g, place: (g, 0, place[1])),
-                pl.BlockSpec((GROUP, row_count, LANES), lambda g, place: (g, 0, place[0])),
-            ],
+            grid=(groups,),
+            in_specs=[table_at(1), table_at(0), plane_at(1), plane_at(0)],
             out_specs=(block, block),
         ),
         compiler_params=pltpu.CompilerParams(vmem_limit_bytes=HEAD_VMEM_BYTES),
-        cost_estimate=pl.CostEstimate(flops=2 * 10**9, bytes_accessed=3 * 2**20, transcendentals=0),
+        cost_estimate=pl.CostEstimate(flops=0, bytes_accessed=0, transcendentals=0),
         name="row_modes",
-    )(place, tables, plane, plane)
+    )(place, tables, tables, plane, plane)
 
 
 def col_modes_kernel(table_ref, plane_ref, out_ref):
@@ -150,16 +164,18 @@
             pl.BlockSpec((GROUP, row_count, col_count), lambda g: (g, 0, 0)),
         ],
         out_specs=pl.BlockSpec((modes, GROUP * row_count), lambda g: (0, g)),
-        compiler_params=pltpu.CompilerParams(vmem_limit_bytes=VMEM_BYTES),
-        cost_estimate=pl.CostEstimate(flops=10**9, bytes_accessed=3 * 2**20, transcendentals=0),
+        compiler_params=pltpu.CompilerParams(vmem_limit_bytes=HEAD_VMEM_BYTES),
+        cost_estimate=pl.CostEstimate(flops=0, bytes_accessed=0, transcendentals=0),
         name="col_modes",
     )(table, plane)
 
 
 def finish_kernel(
     row_scale,
+    paired,
     place_ref,
     modes_ref,
+    more_ref,
     mix_ref,
     inverse_ref,
     local_ref,
@@ -171,13 +187,23 @@
     order_ref,
     *rest,
 ):
-    out_ref, mixed_ref, pre_ref, done_ref, wide_ref = rest[-5:]
-    mode_rows, channels, _ = modes_ref.shape
-    row_count = plane_ref.shape[0]
-    for k in range(mode_rows // 2):
-        pair = modes_ref[2 * k : 2 * k + 2].reshape(2 * channels, LANES)
-        mixed = jnp.dot(mix_ref[k], pair, preferred_element_type=jnp.float32) * row_scale
-        mixed_ref[2 * k : 2 * k + 2] = mixed.astype(jnp.bfloat16).reshape(2, channels, LANES)
+    out_ref, mixed_ref, pre_ref, done_ref, rows_ref, wide_ref = rest[-6:]
+    mode_rows, channels, _ = mixed_ref.shape
+    row_count = plane_ref.shape[1]
+    held = modes_ref.shape[0] // 2
+    for which, source in enumerate((modes_ref,) if paired else (modes_ref, more_ref)):
+        start = 0 if paired else place_ref[which] * held
+        for k in range(held):
+            pair = source[2 * k : 2 * k + 2].reshape(2 * channels, LANES)
+            mixed = jnp.dot(mix_ref[start + k], pair, preferred_element_type=jnp.float32)
+            mixed = (mixed * row_scale).astype(jnp.bfloat16)
+            mixed_ref[pl.ds(2 * (start + k), 2)] = mixed.reshape(2, channels, LANES)
+    for g in range(channels // GROUP):
+        for h in range(row_count // GROUP):
+            o, x = slice(g * GROUP, (g + 1) * GROUP), slice(h * GROUP, (h + 1) * GROUP)
+            block = plane_ref[o, x, :].reshape(GROUP * GROUP, LANES)
+            turned = jnp.dot(order_ref[...], block, preferred_element_type=jnp.float32)
+            rows_ref[x, o, :] = turned.astype(jnp.bfloat16).reshape(GROUP, GROUP, LANES)
     for g in range(channels // GROUP):
         part = mixed_ref[:, g * GROUP : (g + 1) * GROUP, :].reshape(mode_rows * GROUP, LANES)
         rows = jnp.dot(inverse_ref[0], part, preferred_element_type=jnp.float32)
@@ -185,7 +211,7 @@
     cols = col_ref[...]
 
     def one_row(x):
-        data = jnp.concatenate([plane_ref[x], cols], axis=0)
+        data = jnp.concatenate([rows_ref[x], cols], axis=0)
         local = jnp.dot(local_ref[x], data, preferred_element_type=jnp.float32)
         return (pre_ref[x] + local).astype(jnp.bfloat16)
 
@@ -224,21 +250,29 @@
             out_ref[o, x, :] = turned.astype(jnp.bfloat16).reshape(GROUP, GROUP, LANES)
 
 
-def finish(place, which, modes, shared, plane_rows, col_inverse, row_scale, out):
+def finish(place, base, which, modes, more, shared, plane, col_inverse, row_scale, out):
+    paired = more is None
+    more = modes if paired else more
+    mode_rows = modes.shape[0] * (1 if paired else 2)
+
+    def at(place):
+        return base + place[which] if paired else base
+
     mix, inverse, local, up, down, down_bias, order = shared
-    row_count, channels, col_count = plane_rows.shape
+    channels, row_count, col_count = plane.shape
 
     def whole(a):
         return pl.BlockSpec(a.shape, lambda i, place: (0,) * a.ndim)
 
-    operands = [modes, mix, inverse, local, plane_rows, col_inverse, up, down, down_bias, order]
+    operands = [modes, more, mix, inverse, local, plane, col_inverse, up, down, down_bias, order]
     in_specs = [
         whole(modes),
+        pl.BlockSpec(memory_space=pl.ANY) if paired else whole(more),
         whole(mix),
         pl.BlockSpec((1,) + inverse.shape[1:], lambda i, place: (place[2], 0, 0)),
         whole(local),
-        pl.BlockSpec((row_count, channels, LANES), lambda i, place: (0, 0, place[which])),
-        pl.BlockSpec((col_inverse.shape[0], LANES), lambda i, place: (0, place[which])),
+        pl.BlockSpec((channels, row_count, LANES), lambda i, place: (0, 0, at(place))),
+        pl.BlockSpec((col_inverse.shape[0], LANES), lambda i, place: (0, at(place))),
         whole(up),
         whole(down),
         whole(down_bias),
@@ -251,7 +285,7 @@
         aliases = {len(operands): 0}
 
     def kernel(*refs):
-        finish_kernel(row_scale, *refs)
+        finish_kernel(row_scale, paired, *refs)
 
     return pl.pallas_call(
         kernel,
@@ -260,17 +294,18 @@
             num_scalar_prefetch=1,
             grid=(1,),
             in_specs=in_specs,
-            out_specs=pl.BlockSpec((channels, row_count, LANES), lambda i, place: (0, 0, place[which])),
+            out_specs=pl.BlockSpec((channels, row_count, LANES), lambda i, place: (0, 0, at(place))),
             scratch_shapes=[
-                pltpu.VMEM(modes.shape, jnp.bfloat16),
+                pltpu.VMEM((mode_rows, channels, LANES), jnp.bfloat16),
                 pltpu.VMEM((row_count, channels, LANES), jnp.float32),
+                pltpu.VMEM((row_count, channels, LANES), jnp.bfloat16),
                 pltpu.VMEM((row_count, channels, LANES), jnp.bfloat16),
                 pltpu.VMEM((channels+BIAS_ROWS, row_count * LANES), jnp.bfloat16),
             ],
         ),
         input_output_aliases=aliases,
         compiler_params=pltpu.CompilerParams(vmem_limit_bytes=VMEM_BYTES),
-        cost_estimate=pl.CostEstimate(flops=5 * 10**9, bytes_accessed=4 * 2**20, transcendentals=2 * 10**6),
+        cost_estimate=pl.CostEstimate(flops=0, bytes_accessed=0, transcendentals=0),
         name="finish",
     )(place, *operands)
 
@@ -307,19 +342,16 @@
     share = lax.axis_index("gx")
     line = shares == 4
     inner = jnp.where((share == 1) | (share == 2), 1, 0) if line else jnp.zeros((), jnp.int32)
-    rounds = col_count // (2 * LANES)
-    places = [
-        jnp.stack([2 * r + inner, 2 * r + 1 - inner, share]).astype(jnp.int32) for r in range(rounds)
-    ]
+    place = jnp.stack([inner, 1 - inner, share]).astype(jnp.int32)
+    blocks = col_count // LANES
+    rounds = [(i, True) for i in range(0, blocks, 2)]
     tables = row_tables(mode_count, shares, row_count)
 
-    partial = [row_modes(places[r], tables, plane_input, mode_count) for r in range(rounds)]
+    partial = [row_modes(place, tables, plane_input, mode_count, *r) for r in rounds]
     if line:
         near = [lax.ppermute(send, "gx", NEAR) for send, _ in partial]
         half = [add(keep, got) for (_, keep), got in zip(partial, near)]
         far = [lax.ppermute(value, "gx", FAR) for value in half]
-        own = [add(value, got) for value, got in zip(half, far)]
-        other = [lax.ppermute(value, "gx", NEAR) for value in own]
     else:
         own = [lax.psum(keep.astype(jnp.float32), "gx").astype(jnp.bfloat16) for _, keep in partial]
         other = [lax.psum(send.astype(jnp.float32), "gx").astype(jnp.bfloat16) for send, _ in partial]
@@ -328,6 +360,9 @@
     col_offset = lax.axis_index("gy") * col_count
     col_partial = col_modes(forward_table(mode_count, col_total, col_offset, col_count), plane_input)
     col_spectrum = sum_over_cols_axis(col_partial)
+    if line:
+        mine, col_spectrum = lax.optimization_barrier((add(half[0], far[0]), col_spectrum))
+        theirs = lax.ppermute(mine, "gx", NEAR)
     col_spectrum = col_spectrum.astype(jnp.bfloat16).reshape(mode_count, 2 * channels, row_count)
     col_mixed = jnp.einsum(
         "koc,kcx->kox", col_mix, col_spectrum, preferred_element_type=jnp.float32
@@ -357,11 +392,23 @@
         jnp.broadcast_to(down_bias[:, None], (channels, LANES)),
         order,
     )
-    plane_rows = plane_input.transpose(1, 0, 2)
     out = None
-    for r in range(rounds):
-        for which, modes in ((0, own[r]), (1, other[r])):
-            out = finish(places[r], which, modes, shared, plane_rows, col_inverse, row_scale, out)
+    common = (shared, plane_input, col_inverse, row_scale)
+    if line:
+        for i, (base, paired) in enumerate(rounds):
+            out = finish(place, base, 0, mine, None, *common, out)
+            if i + 1 < len(rounds):
+                summed, out = lax.optimization_barrier((half[i + 1], out))
+                following = add(summed, far[i + 1])
+                sent = lax.ppermute(following, "gx", NEAR)
+                out = finish(place, base, 1, theirs, None, *common, out)
+                mine, theirs = following, sent
+            else:
+                out = finish(place, base, 1, theirs, None, *common, out)
+    else:
+        for (base, paired), mine, theirs in zip(rounds, own, other):
+            out = finish(place, base, 0, mine, None, *common, out)
+            out = finish(place, base, 1, theirs, None, *common, out)
     return out
 
 

time: 105 us -> 92.3 us (0.88)
  starting transfers between devices: 43.5 us -> 30.5 us
  waiting for transfers between devices: 1.82 us -> 4.48 us
  other arithmetic: 11.5 us -> 9.13 us
  local copies, waits for them, and re-layouts: 9.68 us -> 7.92 us
  Pallas kernels: 35.6 us -> 37.3 us
    ppermute x2, starting transfers between devices: 31 us -> 2.3 us  [the longest x1 1.61 us: body(): theirs = lax.ppermute(mine, 'gx', NEAR)]
    ppermute x2, starting transfers between devices: 7.42 us -> 23.5 us  [body(): far = [lax.ppermute(value, 'gx', FAR) for value in half]]
    unnamed x36 -> x31, local copies, waits for them, and re-layouts: 6.04 us -> 0.8 us
    ppermute x2, waiting for transfers between devices: 0.01 us -> 3.97 us  [body(): near = [lax.ppermute(send, 'gx', NEAR) for send, _ in partial]]
    pallas_call x1, Pallas kernels: 1.11 us -> 3.9 us  [col_modes(): pl.pallas_call(col_modes_kernel, out_shape=jax.ShapeDtypeStruct((modes, c...]
    pallas_call x2, Pallas kernels: 9.61 us -> 7.29 us  [row_modes(): pl.pallas_call(row_modes_kernel, out_shape=(shape, shape), grid_spec=pltp...]
    ppermute x2, waiting for transfers between devices: 1.81 us -> 0.01 us  [sum_over_cols_axis(): lax.ppermute(value, 'gy', [(i, i ^ step) for i in range(size)])]
    reshape x2, local copies, waits for them, and re-layouts: 1.18 us -> 2.82 us  [body(): col_mixed.reshape(2 * mode_count, channels, row_count).transpose(2, 1, 0)]
  transfers between devices with their start and end apart: 8 -> 8, of which waited for: 1 -> 2; matrix products, arithmetic and copies ran while one was open for 19% -> 20% of each run, Pallas kernels for 24% -> 30%
where the time goes in v2:
time: 92.3 us; the launch traced here: 91.4 us
  Pallas kernels  37.3 us (40%)
  starting transfers between devices  30.5 us (33%)
  other arithmetic  9.13 us (10%)
  local copies, waits for them, and re-layouts  7.92 us (9%)
  waiting for transfers between devices  4.48 us (5%)
  matrix products  1.76 us (2%)
    pallas_call x4, Pallas kernels, finish(): pl.pallas_call(kernel, out_shape=jax.ShapeDtypeStruct((channels, row_coun...  25.4 us
    ppermute x2, starting transfers between devices, body(): far = [lax.ppermute(value, 'gx', FAR) for value in half]  23.5 us
    pallas_call x2, Pallas kernels, row_modes(): pl.pallas_call(row_modes_kernel, out_shape=(shape, shape), grid_spec=pltp...  7.29 us
    convert_element_type x4, other arithmetic, add(): return (a.astype(jnp.float32) + b.astype(jnp.float32)).astype(jnp.bfloat16)  4.83 us
    ppermute x2, waiting for transfers between devices, body(): near = [lax.ppermute(send, 'gx', NEAR) for send, _ in partial]  3.97 us
    pallas_call x1, Pallas kernels, col_modes(): pl.pallas_call(col_modes_kernel, out_shape=jax.ShapeDtypeStruct((modes, c...  3.9 us
    ppermute x2, starting transfers between devices, body(): near = [lax.ppermute(send, 'gx', NEAR) for send, _ in partial]  3.07 us
    reshape x2, local copies, waits for them, and re-layouts, body(): col_mixed.reshape(2 * mode_count, channels, row_count).transpose(2, 1, 0)  2.82 us
  transfers between devices with their start and end apart: 8, of which 2 were waited for; matrix products, arithmetic and copies ran while one was open for 20% of the time, Pallas kernels for 30%

profile of v2, /device:TPU:0, one launch (start us, length us, event | category | flops | bytes accessed | tf_op | source)
XLA Modules:
  0.0 91.4 jit_solution(11787829699586023122)
XLA Ops:
  0.0 0.7 pad_add_fusion.place_ref.refs_0_
  0.7 3.6 %row_modes.3 = (bf16[32,64,128]{2,1,0:T(8,128)(2,1)}, bf16[32,64,128]{2,1,0:T(8,128)(2,1)}) custom-call(s32[3]{0:T(128)} %pad_add_fusion.place_ref.refs_0_, bf16[4,256,256]{2,1,0:T(8,128)(2,1)} %constant.50.clone.refs_0_.refs_1_, bf16[4,256,256]{2,1,0:T(8,128)(2,1)} %constant.50.clone.refs_0_.refs_1_, bf16[64,32,512]{2,1,0:T(8,128)(2,1)} %refs_6_.7, ...), custom_call_target="tpu_custom_call" | custom-call | tf_op jit(solution)/shard_map/row_modes/pallas_call | solution.py:133
  4.2 3.0 %collective-permute-start.1 = (bf16[32,64,128]{2,1,0:T(8,128)(2,1)}, bf16[32,64,128]{2,1,0:T(8,128)(2,1)}, u32[]{:S(2)}, u32[]{:S(2)}) collective-permute-start(bf16[32,64,128]{2,1,0:T(8,128)(2,1)} %get-tuple-element.18), channel_id=1, source_target_pairs={{0,4},{4,0},{8,12},{12,8},{1,5},{5,1},{9,13},{13,9},{2,6},{6,2},{1... | collective-permute-start | bytes 1572872 | tf_op jit(solution)/shard_map/ppermute | solution.py:352
  7.3 0.2 multiply_convert_fusion.1
  7.5 0.6 convert_element_type.84.table_ref
  8.1 3.9 %col_modes.1 = f32[32,2048]{1,0:T(8,128)} custom-call(bf16[32,512]{1,0:T(8,128)(2,1)} %convert_element_type.84.table_ref, bf16[64,32,512]{2,1,0:T(8,128)(2,1)} %refs_6_.7), custom_call_target="tpu_custom_call" | custom-call | tf_op jit(solution)/shard_map/col_modes/pallas_call | solution.py:158
  12.0 0.0 copy-start.11
  12.0 0.1 collective-permute-start.3
  12.1 3.7 %row_modes.2 = (bf16[32,64,128]{2,1,0:T(8,128)(2,1)}, bf16[32,64,128]{2,1,0:T(8,128)(2,1)}) custom-call(s32[3]{0:T(128)} %pad_add_fusion.place_ref.refs_0_, bf16[4,256,256]{2,1,0:T(8,128)(2,1)} %constant.50.clone.refs_0_.refs_1_, bf16[4,256,256]{2,1,0:T(8,128)(2,1)} %constant.50.clone.refs_0_.refs_1_, bf16[64,32,512]{2,1,0:T(8,128)(2,1)} %refs_6_.7, ...), custom_call_target="tpu_custom_call" | custom-call | tf_op jit(solution)/shard_map/row_modes/pallas_call | solution.py:133
  15.8 0.0 copy-start.8
  15.8 0.0 copy-start.9
  15.8 0.1 collective-permute-start
  15.9 4.0 %collective-permute-done.1 = bf16[32,64,128]{2,1,0:T(8,128)(2,1)} collective-permute-done((bf16[32,64,128]{2,1,0:T(8,128)(2,1)}, bf16[32,64,128]{2,1,0:T(8,128)(2,1)}, u32[]{:S(2)}, u32[]{:S(2)}) %collective-permute-start.1) | collective-permute-done | bytes 524320 | tf_op jit(solution)/shard_map/ppermute | solution.py:352
  19.9 0.0 copy-done.10
  19.9 1.2 %add_convert_fusion.2 = bf16[32,64,128]{2,1,0:T(8,128)(2,1)S(1)} fusion(bf16[32,64,128]{2,1,0:T(8,128)(2,1)} %collective-permute-done.1, bf16[32,64,128]{2,1,0:T(8,128)(2,1)S(1)} %copy-done.10), kind=kLoop, calls=%fused_computation.4 | loop fusion | flops 1048576 | bytes 1572864 | tf_op jit(solution)/shard_map/convert_element_type | solution.py:314
  21.1 4.7 %collective-permute-start.2 = (bf16[32,64,128]{2,1,0:T(8,128)(2,1)S(1)}, bf16[32,64,128]{2,1,0:T(8,128)(2,1)}, u32[]{:S(2)}, u32[]{:S(2)}) collective-permute-start(bf16[32,64,128]{2,1,0:T(8,128)(2,1)S(1)} %add_convert_fusion.2), channel_id=1, source_target_pairs={{0,12},{12,0},{4,8},{8,4},{1,13},{13,1},{5,9},{9,5},{2,14},{14,2},... | collective-permute-start | bytes 1572872 | tf_op jit(solution)/shard_map/ppermute | solution.py:354
  25.8 0.0 copy-done.13
  25.8 0.0 copy-done.12
  25.8 0.7 copy.33
  26.6 0.7 copy.39
  27.4 0.0 copy-done.11
  27.4 0.7 copy.38
  28.1 0.0 copy-done.4
  28.1 0.0 copy-done.5
  28.1 0.7 mix_matrices.1
  28.8 0.0 copy-start.6
  28.8 1.1 %fusion.2.refs_8_ = bf16[256,80]{1,0:T(8,128)(2,1)S(1)} fusion(bf16[256,3]{1,0:T(8,128)(2,1)} %copy.39, bf16[256,64]{1,0:T(8,128)(2,1)} %bitcast.16), kind=kLoop, calls=%fused_computation.9 | loop fusion | flops 122880 | bytes 75264 | tf_op jit(solution)/shard_map/concatenate | solution.py:380
  29.9 0.0 collective-permute-done.3
  30.0 0.0 copy-done.8
  30.0 1.0 %add.65 = f32[32,2048]{1,0:T(8,128)S(1)} add(f32[32,2048]{1,0:T(8,128)S(1)} %copy-done.8, f32[32,2048]{1,0:T(8,128)} %collective-permute-done.3) | non-fusion elementwise | flops 65536 | bytes 786432 | tf_op jit(solution)/shard_map/add | solution.py:327
  30.9 1.6 %collective-permute-start.4 = (f32[32,2048]{1,0:T(8,128)S(1)}, f32[32,2048]{1,0:T(8,128)S(1)}, u32[]{:S(2)}, u32[]{:S(2)}) collective-permute-start(f32[32,2048]{1,0:T(8,128)S(1)} %add.65), channel_id=1, source_target_pairs={{0,2},{1,3},{2,0},{3,1},{4,6},{5,7},{6,4},{7,5},{8,10},{9,11},{10,... | collective-permute-start | bytes 786440 | tf_op jit(solution)/shard_map/ppermute | solution.py:327
  32.5 0.0 collective-permute-done
  32.5 0.0 copy-done.9
  32.5 1.0 %add_convert_fusion.3 = bf16[32,64,128]{2,1,0:T(8,128)(2,1)} fusion(bf16[32,64,128]{2,1,0:T(8,128)(2,1)S(1)} %collective-permute-done, bf16[32,64,128]{2,1,0:T(8,128)(2,1)S(1)} %copy-done.9), kind=kLoop, calls=%fused_computation.5 | loop fusion | flops 1048576 | bytes 1572864 | tf_op jit(solution)/shard_map/convert_element_type | solution.py:314
  33.5 18.8 %collective-permute-start.5 = (bf16[32,64,128]{2,1,0:T(8,128)(2,1)}, bf16[32,64,128]{2,1,0:T(8,128)(2,1)}, u32[]{:S(2)}, u32[]{:S(2)}) collective-permute-start(bf16[32,64,128]{2,1,0:T(8,128)(2,1)} %add_convert_fusion.3), channel_id=1, source_target_pairs={{0,12},{12,0},{4,8},{8,4},{1,13},{13,1},{5,9},{9,5},{2,14},{14,2},... | collective-permute-start | bytes 1572872 | tf_op jit(solution)/shard_map/ppermute | solution.py:354
  52.4 0.0 collective-permute-done.4
  52.4 0.0 copy-done.6
  52.4 0.0 collective-permute-done.2
  52.4 1.2 %add_convert_fusion.1.refs_1_.refs_2_ = bf16[32,64,128]{2,1,0:T(8,128)(2,1)S(1)} fusion(bf16[32,64,128]{2,1,0:T(8,128)(2,1)} %collective-permute-done.2, bf16[32,64,128]{2,1,0:T(8,128)(2,1)S(1)} %add_convert_fusion.2), kind=kLoop, calls=%fused_computation.3 | loop fusion | flops 1048576 | bytes 1572864 | tf_op jit(solution)/shard_map/convert_element_type | solution.py:314
  53.7 1.2 %reshape.205 = bf16[16,128,32]{2,1,0:T(8,128)(2,1)} reshape(bf16[32,2048]{1,0:T(8,128)(2,1)S(1)} %add.66) | data formatting | bytes 262144 | tf_op jit(solution)/shard_map/reshape | solution.py:366
  54.8 0.0 copy-start.7
  54.8 1.8 %fusion = bf16[16,128,32]{1,2,0:T(8,128)(2,1)S(1)} fusion(bf16[16,128,128]{2,1,0:T(8,128)(2,1)} %copy-done.6, bf16[16,128,32]{2,1,0:T(8,128)(2,1)} %reshape.205), kind=kOutput, calls=%fused_computation.1 | convolution fusion | flops 16908288 | bytes 786432 | tf_op jit(solution)/shard_map/koc,kcx->kox/dot_general | solution.py:367
  56.6 0.1 copy.35
  56.7 0.9 reshape.206
  57.5 2.0 %copy.36 = bf16[32,64,32]{0,1,2:T(8,128)(2,1)} copy(bf16[32,64,32]{1,0,2:T(8,128)(2,1)} %reshape.206) | data formatting | bytes 262144 | tf_op jit(solution)/shard_map/reshape | solution.py:371
  59.5 1.6 %collective-permute-start.7 = (bf16[32,64,128]{2,1,0:T(8,128)(2,1)S(1)}, bf16[32,64,128]{2,1,0:T(8,128)(2,1)S(1)}, u32[]{:S(2)}, u32[]{:S(2)}) collective-permute-start(bf16[32,64,128]{2,1,0:T(8,128)(2,1)S(1)} %add_convert_fusion.1.refs_1_.refs_2_), channel_id=1, source_target_pairs={{0,4},{4,0},{8,12},{12,8},{1,5},{5,1},{9,13},{13,9},{2,6},{6,2},{1... | collective-permute-start | bytes 1572872 | tf_op jit(solution)/shard_map/ppermute | solution.py:365
  61.1 0.8 broadcast_in_dim.12
  61.9 1.3 %pad_maximum_fusion.refs_5_ = bf16[32,64,96]{2,1,0:T(8,128)(2,1)S(1)} fusion(bf16[32,64,32]{2,1,0:T(8,128)(2,1)} %bitcast.15, bf16[32,64,64]{2,1,0:T(8,128)(2,1)S(1)} %broadcast_in_dim.12), kind=kLoop, calls=%fused_computation.6 | loop fusion | flops 786432 | bytes 786432 | tf_op jit(solution)/shard_map/concatenate | solution.py:373
  63.3 0.0 copy-done.14
  63.3 0.1 broadcast_in_dim.15.refs_10_
  63.4 0.0 copy-done
  63.4 0.0 copy-done.2
  63.4 0.0 copy-done.3
  63.4 0.0 copy-done.7
  63.4 0.0 copy-done.1
  63.4 6.3 %finish.4.refs_12_ = bf16[64,32,512]{2,1,0:T(8,128)(2,1)} custom-call(s32[3]{0:T(128)S(1)} %copy-done.7, bf16[32,64,128]{2,1,0:T(8,128)(2,1)S(1)} %add_convert_fusion.1.refs_1_.refs_2_, bf16[32,64,128]{2,1,0:T(8,128)(2,1)S(1)} %add_convert_fusion.1.refs_1_.refs_2_, bf16[16,128,128]{2,1,0:T(8,128)(2,1)S(1)} %get-tuple-element.20.refs_3_, ...), custom_call_target="tpu_custom_call" | custom-call | tf_op jit(solution)/shard_map/finish/pallas_call | solution.py:290
  69.7 0.0 collective-permute-done.5
  69.7 1.4 %add_convert_fusion.refs_1_.refs_2_ = bf16[32,64,128]{2,1,0:T(8,128)(2,1)S(1)} fusion(bf16[32,64,128]{2,1,0:T(8,128)(2,1)} %collective-permute-done.5, bf16[32,64,128]{2,1,0:T(8,128)(2,1)} %add_convert_fusion.3), kind=kLoop, calls=%fused_computation.2 | loop fusion | flops 1048576 | bytes 1572864 | tf_op jit(solution)/shard_map/convert_element_type | solution.py:314
  71.1 0.7 collective-permute-start.6
  71.8 0.5 collective-permute-done.7.refs_1_.refs_2_
  72.3 6.5 %finish.5.refs_12_ = bf16[64,32,512]{2,1,0:T(8,128)(2,1)} custom-call(s32[3]{0:T(128)S(1)} %copy-done.7, bf16[32,64,128]{2,1,0:T(8,128)(2,1)S(1)} %collective-permute-done.7.refs_1_.refs_2_, bf16[32,64,128]{2,1,0:T(8,128)(2,1)S(1)} %collective-permute-done.7.refs_1_.refs_2_, ...), custom_call_target="tpu_custom_call", output_to_operand_aliasing={{}: (12, {})} | custom-call | tf_op jit(solution)/shard_map/finish/pallas_call | solution.py:290
  78.8 6.3 %finish.6.refs_12_ = bf16[64,32,512]{2,1,0:T(8,128)(2,1)} custom-call(s32[3]{0:T(128)S(1)} %copy-done.7, bf16[32,64,128]{2,1,0:T(8,128)(2,1)S(1)} %add_convert_fusion.refs_1_.refs_2_, bf16[32,64,128]{2,1,0:T(8,128)(2,1)S(1)} %add_convert_fusion.refs_1_.refs_2_, bf16[16,128,128]{2,1,0:T(8,128)(2,1)S(1)} %get-tuple-element.20.refs_3_, ...), custom_call_target="tpu_custom_call", output_to_operand_aliasing={{}: (12, {})} | custom-call | tf_op jit(solution)/shard_map/finish/pallas_call | solution.py:290
  85.1 0.0 collective-permute-done.6.refs_1_.refs_2_
  85.1 6.3 %finish.7 = bf16[64,32,512]{2,1,0:T(8,128)(2,1)} custom-call(s32[3]{0:T(128)S(1)} %copy-done.7, bf16[32,64,128]{2,1,0:T(8,128)(2,1)S(1)} %collective-permute-done.6.refs_1_.refs_2_, bf16[32,64,128]{2,1,0:T(8,128)(2,1)S(1)} %collective-permute-done.6.refs_1_.refs_2_, ...), custom_call_target="tpu_custom_call", output_to_operand_aliasing={{}: (12, {})} | custom-call | tf_op jit(solution)/shard_map/finish/pallas_call | solution.py:290
  (23 shorter events, 0.2 us)
Async XLA Ops:
  4.2 15.6 %collective-permute-start.1 = (bf16[32,64,128]{2,1,0:T(8,128)(2,1)}, bf16[32,64,128]{2,1,0:T(8,128)(2,1)}, u32[]{:S(2)}, u32[]{:S(2)}) collective-permute-start(bf16[32,64,128]{2,1,0:T(8,128)(2,1)} %get-tuple-element.18), channel_id=1, source_target_pairs={{0,4},{4,0},{8,12},{12,8},{1,5},{5,1},{9,13},{13,9},{2,6},{6,2},{1... | collective-permute-start | bytes 1572872 | tf_op jit(solution)/shard_map/ppermute | solution.py:352
  12.0 7.9 %copy-start.10 = (bf16[32,64,128]{2,1,0:T(8,128)(2,1)S(1)}, bf16[32,64,128]{2,1,0:T(8,128)(2,1)}, u32[]{:S(2)}) copy-start(bf16[32,64,128]{2,1,0:T(8,128)(2,1)} %get-tuple-element.17) | copy-start | bytes 1572868
  12.0 13.8 %copy-start.13 = (f32[256]{0:T(256)S(1)}, f32[256]{0:T(256)}, u32[]{:S(2)}) copy-start(f32[256]{0:T(256)} %param.16) | copy-start | bytes 3076
  12.0 13.8 %copy-start.12 = (bf16[64,64]{1,0:T(8,128)(2,1)S(1)}, bf16[64,64]{1,0:T(8,128)(2,1)}, u32[]{:S(2)}) copy-start(bf16[64,64]{1,0:T(8,128)(2,1)} %param.14) | copy-start | bytes 24580
  12.0 15.4 %copy-start.11 = (bf16[64,256]{1,0:T(8,128)(2,1)S(1)}, bf16[64,256]{1,0:T(8,128)(2,1)}, u32[]{:S(2)}) copy-start(bf16[64,256]{1,0:T(8,128)(2,1)} %param.15) | copy-start | bytes 98308
  12.0 17.9 %collective-permute-start.3 = (f32[32,2048]{1,0:T(8,128)}, f32[32,2048]{1,0:T(8,128)}, u32[]{:S(2)}, u32[]{:S(2)}) collective-permute-start(f32[32,2048]{1,0:T(8,128)} %col_modes.1), channel_id=1, source_target_pairs={{0,1},{1,0},{2,3},{3,2},{4,5},{5,4},{6,7},{7,6},{8,9},{9,8},{10,11... | collective-permute-start | bytes 786440 | tf_op jit(solution)/shard_map/ppermute | solution.py:327
  15.8 12.3 %copy-start.4 = (bf16[2,16,64,64]{3,2,1,0:T(8,128)(2,1)S(1)}, bf16[2,16,64,64]{3,2,1,0:T(8,128)(2,1)}, u32[]{:S(2)}) copy-start(bf16[2,16,64,64]{3,2,1,0:T(8,128)(2,1)} %row_ref.1) | copy-start | bytes 786436
  15.8 12.3 %copy-start.5 = (bf16[2,16,64,64]{3,2,1,0:T(8,128)(2,1)S(1)}, bf16[2,16,64,64]{3,2,1,0:T(8,128)(2,1)}, u32[]{:S(2)}) copy-start(bf16[2,16,64,64]{3,2,1,0:T(8,128)(2,1)} %col_ref.1) | copy-start | bytes 786436
  15.8 14.1 %copy-start.8 = (f32[32,2048]{1,0:T(8,128)S(1)}, f32[32,2048]{1,0:T(8,128)}, u32[]{:S(2)}) copy-start(f32[32,2048]{1,0:T(8,128)} %col_modes.1) | copy-start | bytes 786436
  15.8 16.7 %copy-start.9 = (bf16[32,64,128]{2,1,0:T(8,128)(2,1)S(1)}, bf16[32,64,128]{2,1,0:T(8,128)(2,1)}, u32[]{:S(2)}) copy-start(bf16[32,64,128]{2,1,0:T(8,128)(2,1)} %get-tuple-element.15) | copy-start | bytes 1572868
  15.8 16.7 %collective-permute-start = (bf16[32,64,128]{2,1,0:T(8,128)(2,1)}, bf16[32,64,128]{2,1,0:T(8,128)(2,1)S(1)}, u32[]{:S(2)}, u32[]{:S(2)}) collective-permute-start(bf16[32,64,128]{2,1,0:T(8,128)(2,1)} %get-tuple-element.16), channel_id=1, source_target_pairs={{0,4},{4,0},{8,12},{12,8},{1,5},{5,1},{9,13},{13,9},{2,6},{6,2},{1... | collective-permute-start | bytes 1572872 | tf_op jit(solution)/shard_map/ppermute | solution.py:352
  21.1 31.3 %collective-permute-start.2 = (bf16[32,64,128]{2,1,0:T(8,128)(2,1)S(1)}, bf16[32,64,128]{2,1,0:T(8,128)(2,1)}, u32[]{:S(2)}, u32[]{:S(2)}) collective-permute-start(bf16[32,64,128]{2,1,0:T(8,128)(2,1)S(1)} %add_convert_fusion.2), channel_id=1, source_target_pairs={{0,12},{12,0},{4,8},{8,4},{1,13},{13,1},{5,9},{9,5},{2,14},{14,2},... | collective-permute-start | bytes 1572872 | tf_op jit(solution)/shard_map/ppermute | solution.py:354
  28.8 23.6 %copy-start.6 = (bf16[16,128,128]{2,1,0:T(8,128)(2,1)}, bf16[16,128,128]{2,1,0:T(8,128)(2,1)S(1)}, u32[]{:S(2)}) copy-start(bf16[16,128,128]{2,1,0:T(8,128)(2,1)S(1)} %get-tuple-element.21) | copy-start | bytes 1572868
  30.9 21.4 %collective-permute-start.4 = (f32[32,2048]{1,0:T(8,128)S(1)}, f32[32,2048]{1,0:T(8,128)S(1)}, u32[]{:S(2)}, u32[]{:S(2)}) collective-permute-start(f32[32,2048]{1,0:T(8,128)S(1)} %add.65), channel_id=1, source_target_pairs={{0,2},{1,3},{2,0},{3,1},{4,6},{5,7},{6,4},{7,5},{8,10},{9,11},{10,... | collective-permute-start | bytes 786440 | tf_op jit(solution)/shard_map/ppermute | solution.py:327
  33.5 36.2 %collective-permute-start.5 = (bf16[32,64,128]{2,1,0:T(8,128)(2,1)}, bf16[32,64,128]{2,1,0:T(8,128)(2,1)}, u32[]{:S(2)}, u32[]{:S(2)}) collective-permute-start(bf16[32,64,128]{2,1,0:T(8,128)(2,1)} %add_convert_fusion.3), channel_id=1, source_target_pairs={{0,12},{12,0},{4,8},{8,4},{1,13},{13,1},{5,9},{9,5},{2,14},{14,2},... | collective-permute-start | bytes 1572872 | tf_op jit(solution)/shard_map/ppermute | solution.py:354
  54.8 8.5 %copy-start.14 = (f32[64]{0:T(128)S(1)}, f32[64]{0:T(128)}, u32[]{:S(2)}) copy-start(f32[64]{0:T(128)} %param.18) | copy-start | bytes 772
  54.8 8.5 %copy-start = (bf16[64,32,512]{2,1,0:T(8,128)(2,1)S(1)}, bf16[64,32,512]{2,1,0:T(8,128)(2,1)}, u32[]{:S(2)}) copy-start(bf16[64,32,512]{2,1,0:T(8,128)(2,1)} %refs_6_.7) | copy-start | bytes 6291460
  54.8 8.5 %copy-start.2 = (bf16[256,256]{1,0:T(8,128)(2,1)S(1)}, bf16[256,256]{1,0:T(8,128)(2,1)}, u32[]{:S(2)}) copy-start(bf16[256,256]{1,0:T(8,128)(2,1)} %constant.51.clone.refs_11_) | copy-start | bytes 393220
  54.8 8.5 %copy-start.3 = (bf16[256,64]{0,1:T(8,128)(2,1)S(1)}, bf16[256,64]{0,1:T(8,128)(2,1)}, u32[]{:S(2)}) copy-start(bf16[256,64]{0,1:T(8,128)(2,1)} %param.17) | copy-start | bytes 98308
  54.8 8.5 %copy-start.7 = (s32[3]{0:T(128)S(1)}, s32[3]{0:T(128)}, u32[]{:S(2)}) copy-start(s32[3]{0:T(128)} %pad_add_fusion.place_ref.refs_0_) | copy-start | bytes 40
  59.5 3.9 %copy-start.1 = (bf16[4,512,512]{2,1,0:T(8,128)(2,1)S(1)}, bf16[4,512,512]{2,1,0:T(8,128)(2,1)}, u32[]{:S(2)}) copy-start(bf16[4,512,512]{2,1,0:T(8,128)(2,1)} %constant.52.clone.refs_4_) | copy-start | bytes 6291460
  59.5 12.8 %collective-permute-start.7 = (bf16[32,64,128]{2,1,0:T(8,128)(2,1)S(1)}, bf16[32,64,128]{2,1,0:T(8,128)(2,1)S(1)}, u32[]{:S(2)}, u32[]{:S(2)}) collective-permute-start(bf16[32,64,128]{2,1,0:T(8,128)(2,1)S(1)} %add_convert_fusion.1.refs_1_.refs_2_), channel_id=1, source_target_pairs={{0,4},{4,0},{8,12},{12,8},{1,5},{5,1},{9,13},{13,9},{2,6},{6,2},{1... | collective-permute-start | bytes 1572872 | tf_op jit(solution)/shard_map/ppermute | solution.py:365
  71.1 14.0 %collective-permute-start.6 = (bf16[32,64,128]{2,1,0:T(8,128)(2,1)S(1)}, bf16[32,64,128]{2,1,0:T(8,128)(2,1)S(1)}, u32[]{:S(2)}, u32[]{:S(2)}) collective-permute-start(bf16[32,64,128]{2,1,0:T(8,128)(2,1)S(1)} %add_convert_fusion.refs_1_.refs_2_), channel_id=1, source_target_pairs={{0,4},{4,0},{8,12},{12,8},{1,5},{5,1},{9,13},{13,9},{2,6},{6,2},{1... | collective-permute-start | bytes 1572872 | tf_op jit(solution)/shard_map/ppermute | solution.py:403

commit v3 on v2

--- a/solution.py
+++ b/solution.py
@@ -97,8 +97,8 @@
     )(row_weight, col_weight)
 
 
-def row_modes_kernel(place_ref, *refs):
-    for table, source, target in zip(refs[0:2], refs[2:4], refs[4:6]):
+def row_modes_kernel(place_ref, table, *refs):
+    for source, target in zip(refs[:2], refs[2:]):
         for g in range(source.shape[0] // GROUP):
             parts = []
             for half in range(2):
@@ -110,24 +110,20 @@
             target[:, at, :] = jnp.concatenate(parts, axis=1).astype(jnp.bfloat16)
 
 
-def row_modes(place, tables, plane, mode_count, base, paired):
+def row_modes(place, tables, plane, mode_count, base):
     channels, row_count, _ = plane.shape
-    modes = 2 * mode_count if paired else mode_count
+    modes = 2 * mode_count
     groups = channels // STEP_CHANNELS
     shape = jax.ShapeDtypeStruct((modes, channels, LANES), jnp.bfloat16)
     block = pl.BlockSpec((modes, STEP_CHANNELS, LANES), lambda g, place: (0, g, 0))
     rows = modes * HALF_GROUP
 
-    def table_at(which):
-        return pl.BlockSpec(
-            (1, rows, tables.shape[2]),
-            lambda g, place: (place[2], 0 if paired else place[which], 0),
-        )
+    table_at = pl.BlockSpec((1, rows, tables.shape[2]), lambda g, place: (place[2], 0, 0))
 
     def plane_at(which):
         return pl.BlockSpec(
             (STEP_CHANNELS, row_count, LANES),
-            lambda g, place: (g, 0, base + place[which] if paired else base),
+            lambda g, place: (g, 0, base + place[which]),
         )
 
     return pl.pallas_call(
@@ -136,13 +132,13 @@
         grid_spec=pltpu.PrefetchScalarGridSpec(
             num_scalar_prefetch=1,
             grid=(groups,),
-            in_specs=[table_at(1), table_at(0), plane_at(1), plane_at(0)],
+            in_specs=[table_at, plane_at(1), plane_at(0)],
             out_specs=(block, block),
         ),
         compiler_params=pltpu.CompilerParams(vmem_limit_bytes=HEAD_VMEM_BYTES),
         cost_estimate=pl.CostEstimate(flops=0, bytes_accessed=0, transcendentals=0),
         name="row_modes",
-    )(place, tables, tables, plane, plane)
+    )(place, tables, plane, plane)
 
 
 def col_modes_kernel(table_ref, plane_ref, out_ref):
@@ -172,7 +168,7 @@
 
 def finish_kernel(
     row_scale,
-    paired,
+    single,
     place_ref,
     modes_ref,
     more_ref,
@@ -190,14 +186,19 @@
     out_ref, mixed_ref, pre_ref, done_ref, rows_ref, wide_ref = rest[-6:]
     mode_rows, channels, _ = mixed_ref.shape
     row_count = plane_ref.shape[1]
-    held = modes_ref.shape[0] // 2
-    for which, source in enumerate((modes_ref,) if paired else (modes_ref, more_ref)):
-        start = 0 if paired else place_ref[which] * held
-        for k in range(held):
+
+    def mix(source):
+        for k in range(mode_rows // 2):
             pair = source[2 * k : 2 * k + 2].reshape(2 * channels, LANES)
-            mixed = jnp.dot(mix_ref[start + k], pair, preferred_element_type=jnp.float32)
+            mixed = jnp.dot(mix_ref[k], pair, preferred_element_type=jnp.float32)
             mixed = (mixed * row_scale).astype(jnp.bfloat16)
-            mixed_ref[pl.ds(2 * (start + k), 2)] = mixed.reshape(2, channels, LANES)
+            mixed_ref[2 * k : 2 * k + 2] = mixed.reshape(2, channels, LANES)
+
+    if single:
+        mix(modes_ref)
+    else:
+        pl.when(pl.program_id(0) == 0)(lambda: mix(modes_ref))
+        pl.when(pl.program_id(0) == 1)(lambda: mix(more_ref))
     for g in range(channels // GROUP):
         for h in range(row_count // GROUP):
             o, x = slice(g * GROUP, (g + 1) * GROUP), slice(h * GROUP, (h + 1) * GROUP)
@@ -250,15 +251,17 @@
             out_ref[o, x, :] = turned.astype(jnp.bfloat16).reshape(GROUP, GROUP, LANES)
 
 
-def finish(place, base, which, modes, more, shared, plane, col_inverse, row_scale, out):
-    paired = more is None
-    more = modes if paired else more
-    mode_rows = modes.shape[0] * (1 if paired else 2)
-
-    def at(place):
-        return base + place[which] if paired else base
-
+def finish(place, at, modes, shared, plane, col_inverse, row_scale, out):
     mix, inverse, local, up, down, down_bias, order = shared
+    single = len(modes) == 1
+    modes, more = modes[0], modes[-1]
+    mode_rows = modes.shape[0]
+
+    def column(i, place):
+        (base, which), (last_base, last_which) = at[0], at[-1]
+        first = base + place[which]
+        return first if single else jnp.where(i == 0, first, last_base + place[last_which])
+
     channels, row_count, col_count = plane.shape
 
     def whole(a):
@@ -267,12 +270,12 @@
     operands = [modes, more, mix, inverse, local, plane, col_inverse, up, down, down_bias, order]
     in_specs = [
         whole(modes),
-        pl.BlockSpec(memory_space=pl.ANY) if paired else whole(more),
+        pl.BlockSpec(memory_space=pl.ANY) if single else whole(more),
         whole(mix),
         pl.BlockSpec((1,) + inverse.shape[1:], lambda i, place: (place[2], 0, 0)),
         whole(local),
-        pl.BlockSpec((channels, row_count, LANES), lambda i, place: (0, 0, at(place))),
-        pl.BlockSpec((col_inverse.shape[0], LANES), lambda i, place: (0, at(place))),
+        pl.BlockSpec((channels, row_count, LANES), lambda i, place: (0, 0, column(i, place))),
+        pl.BlockSpec((col_inverse.shape[0], LANES), lambda i, place: (0, column(i, place))),
         whole(up),
         whole(down),
         whole(down_bias),
@@ -285,16 +288,16 @@
         aliases = {len(operands): 0}
 
     def kernel(*refs):
-        finish_kernel(row_scale, paired, *refs)
+        finish_kernel(row_scale, single, *refs)
 
     return pl.pallas_call(
         kernel,
         out_shape=jax.ShapeDtypeStruct((channels, row_count, col_count), jnp.bfloat16),
         grid_spec=pltpu.PrefetchScalarGridSpec(
             num_scalar_prefetch=1,
-            grid=(1,),
+            grid=(1 if single else 2,),
             in_specs=in_specs,
-            out_specs=pl.BlockSpec((channels, row_count, LANES), lambda i, place: (0, 0, at(place))),
+            out_specs=pl.BlockSpec((channels, row_count, LANES), lambda i, place: (0, 0, column(i, place))),
             scratch_shapes=[
                 pltpu.VMEM((mode_rows, channels, LANES), jnp.bfloat16),
                 pltpu.VMEM((row_count, channels, LANES), jnp.float32),
@@ -344,14 +347,13 @@
     inner = jnp.where((share == 1) | (share == 2), 1, 0) if line else jnp.zeros((), jnp.int32)
     place = jnp.stack([inner, 1 - inner, share]).astype(jnp.int32)
     blocks = col_count // LANES
-    rounds = [(i, True) for i in range(0, blocks, 2)]
+    rounds = list(range(0, blocks, 2))
     tables = row_tables(mode_count, shares, row_count)
 
-    partial = [row_modes(place, tables, plane_input, mode_count, *r) for r in rounds]
+    partial = [row_modes(place, tables, plane_input, mode_count, base) for base in rounds]
     if line:
         near = [lax.ppermute(send, "gx", NEAR) for send, _ in partial]
         half = [add(keep, got) for (_, keep), got in zip(partial, near)]
-        far = [lax.ppermute(value, "gx", FAR) for value in half]
     else:
         own = [lax.psum(keep.astype(jnp.float32), "gx").astype(jnp.bfloat16) for _, keep in partial]
         other = [lax.psum(send.astype(jnp.float32), "gx").astype(jnp.bfloat16) for send, _ in partial]
@@ -361,8 +363,8 @@
     col_partial = col_modes(forward_table(mode_count, col_total, col_offset, col_count), plane_input)
     col_spectrum = sum_over_cols_axis(col_partial)
     if line:
-        mine, col_spectrum = lax.optimization_barrier((add(half[0], far[0]), col_spectrum))
-        theirs = lax.ppermute(mine, "gx", NEAR)
+        half[1], col_spectrum = lax.optimization_barrier((half[1], col_spectrum))
+        far = [lax.ppermute(value, "gx", FAR) for value in half]
     col_spectrum = col_spectrum.astype(jnp.bfloat16).reshape(mode_count, 2 * channels, row_count)
     col_mixed = jnp.einsum(
         "koc,kcx->kox", col_mix, col_spectrum, preferred_element_type=jnp.float32
@@ -395,20 +397,20 @@
     out = None
     common = (shared, plane_input, col_inverse, row_scale)
     if line:
-        for i, (base, paired) in enumerate(rounds):
-            out = finish(place, base, 0, mine, None, *common, out)
-            if i + 1 < len(rounds):
-                summed, out = lax.optimization_barrier((half[i + 1], out))
-                following = add(summed, far[i + 1])
-                sent = lax.ppermute(following, "gx", NEAR)
-                out = finish(place, base, 1, theirs, None, *common, out)
-                mine, theirs = following, sent
-            else:
-                out = finish(place, base, 1, theirs, None, *common, out)
+        waiting = []
+        for i, base in enumerate(rounds):
+            summed = half[i]
+            if out is not None:
+                summed, out = lax.optimization_barrier((summed, out))
+            mine = add(summed, far[i])
+            theirs = lax.ppermute(mine, "gx", NEAR)
+            ready = waiting + [((base, 0), mine)]
+            out = finish(place, [w[0] for w in ready], [w[1] for w in ready], *common, out)
+            waiting = [((base, 1), theirs)]
+        out = finish(place, [waiting[0][0]], [waiting[0][1]], *common, out)
     else:
-        for (base, paired), mine, theirs in zip(rounds, own, other):
-            out = finish(place, base, 0, mine, None, *common, out)
-            out = finish(place, base, 1, theirs, None, *common, out)
+        for base, mine, theirs in zip(rounds, own, other):
+            out = finish(place, [(base, 0), (base, 1)], [mine, theirs], *common, out)
     return out
 
 

time: 92.3 us -> 91.6 us (level)
  starting transfers between devices: 30.5 us -> 34 us
  local copies, waits for them, and re-layouts: 7.92 us -> 5.77 us
  matrix products: 1.76 us -> 0.41 us
  Pallas kernels: 37.3 us -> 36.3 us
    ppermute x1 -> x2, starting transfers between devices: 1.61 us -> 4.97 us  [body(): theirs = lax.ppermute(mine, 'gx', NEAR)]
    ppermute x2, waiting for transfers between devices: 0.01 us -> 1.73 us  [sum_over_cols_axis(): lax.ppermute(value, 'gy', [(i, i ^ step) for i in range(size)])]
    dot_general x1, matrix products: 1.76 us -> 0.41 us  [body(): jnp.einsum('koc,kcx->kox', col_mix, col_spectrum, preferred_element_type=...]
    convert_element_type x4, other arithmetic: 4.83 us -> 5.87 us  [add(): return (a.astype(jnp.float32) + b.astype(jnp.float32)).astype(jnp.bfloat16)]
    concatenate x1, other arithmetic: 1.11 us -> 0.09 us  [body(): up = jnp.concatenate([up_weight.T, bias_part], axis=1)]
    pallas_call x4 -> x3, Pallas kernels: 25.4 us -> 24.6 us  [finish(): pl.pallas_call(kernel, out_shape=jax.ShapeDtypeStruct((channels, row_coun...]
  transfers between devices with their start and end apart: 8 -> 8, of which waited for: 2 -> 2; matrix products, arithmetic and copies ran while one was open for 20% -> 15% of each run, Pallas kernels for 30% -> 29%
where the time goes in v3:
time: 91.6 us; the launch traced here: 91.1 us
  Pallas kernels  36.3 us (40%)
  starting transfers between devices  34 us (37%)
  other arithmetic  9.31 us (10%)
  local copies, waits for them, and re-layouts  5.77 us (6%)
  waiting for transfers between devices  5.01 us (5%)
    pallas_call x3, Pallas kernels, finish(): pl.pallas_call(kernel, out_shape=jax.ShapeDtypeStruct((channels, row_coun...  24.6 us
    ppermute x2, starting transfers between devices, body(): far = [lax.ppermute(value, 'gx', FAR) for value in half]  24 us
    pallas_call x2, Pallas kernels, row_modes(): pl.pallas_call(row_modes_kernel, out_shape=(shape, shape), grid_spec=pltp...  7.13 us
    convert_element_type x4, other arithmetic, add(): return (a.astype(jnp.float32) + b.astype(jnp.float32)).astype(jnp.bfloat16)  5.87 us
    ppermute x2, starting transfers between devices, body(): theirs = lax.ppermute(mine, 'gx', NEAR)  4.97 us
    pallas_call x1, Pallas kernels, col_modes(): pl.pallas_call(col_modes_kernel, out_shape=jax.ShapeDtypeStruct((modes, c...  3.92 us
    ppermute x2, waiting for transfers between devices, body(): near = [lax.ppermute(send, 'gx', NEAR) for send, _ in partial]  3.27 us
    ppermute x2, starting transfers between devices, body(): near = [lax.ppermute(send, 'gx', NEAR) for send, _ in partial]  3.05 us
  transfers between devices with their start and end apart: 8, of which 2 were waited for; matrix products, arithmetic and copies ran while one was open for 15% of the time, Pallas kernels for 29%

profile of v3, /device:TPU:0, one launch (start us, length us, event | category | flops | bytes accessed | tf_op | source)
XLA Modules:
  0.0 91.1 jit_solution(8369780098538026642)
XLA Ops:
  0.0 0.6 pad_add_fusion.place_ref.refs_0_
  0.6 3.5 %row_modes.3 = (bf16[32,64,128]{2,1,0:T(8,128)(2,1)}, bf16[32,64,128]{2,1,0:T(8,128)(2,1)}) custom-call(s32[3]{0:T(128)} %pad_add_fusion.place_ref.refs_0_, bf16[4,256,256]{2,1,0:T(8,128)(2,1)} %constant.50.clone.table, bf16[64,32,512]{2,1,0:T(8,128)(2,1)} %refs_6_.5, bf16[64,32,512]{2,1,0:T(8,128)(2,1)} %refs_6_.5), custom_call_target="tpu_custom_call" | custom-call | tf_op jit(solution)/shard_map/row_modes/pallas_call | solution.py:129
  4.1 3.0 %collective-permute-start.3 = (bf16[32,64,128]{2,1,0:T(8,128)(2,1)}, bf16[32,64,128]{2,1,0:T(8,128)(2,1)}, u32[]{:S(2)}, u32[]{:S(2)}) collective-permute-start(bf16[32,64,128]{2,1,0:T(8,128)(2,1)} %get-tuple-element.19), channel_id=1, source_target_pairs={{0,4},{4,0},{8,12},{12,8},{1,5},{5,1},{9,13},{13,9},{2,6},{6,2},{1... | collective-permute-start | bytes 1572872 | tf_op jit(solution)/shard_map/ppermute | solution.py:355
  7.1 0.2 multiply_convert_fusion.1
  7.4 0.6 convert_element_type.78.table_ref
  8.0 3.9 %col_modes.1 = f32[32,2048]{1,0:T(8,128)} custom-call(bf16[32,512]{1,0:T(8,128)(2,1)} %convert_element_type.78.table_ref, bf16[64,32,512]{2,1,0:T(8,128)(2,1)} %refs_6_.5), custom_call_target="tpu_custom_call" | custom-call | tf_op jit(solution)/shard_map/col_modes/pallas_call | solution.py:154
  11.9 0.0 copy-start.11
  11.9 0.0 copy-start.10
  11.9 0.0 copy-start.9
  11.9 0.0 copy-start.3
  11.9 0.1 collective-permute-start.1
  12.0 3.6 %row_modes.2 = (bf16[32,64,128]{2,1,0:T(8,128)(2,1)}, bf16[32,64,128]{2,1,0:T(8,128)(2,1)}) custom-call(s32[3]{0:T(128)} %pad_add_fusion.place_ref.refs_0_, bf16[4,256,256]{2,1,0:T(8,128)(2,1)} %constant.50.clone.table, bf16[64,32,512]{2,1,0:T(8,128)(2,1)} %refs_6_.5, bf16[64,32,512]{2,1,0:T(8,128)(2,1)} %refs_6_.5), custom_call_target="tpu_custom_call" | custom-call | tf_op jit(solution)/shard_map/row_modes/pallas_call | solution.py:129
  15.6 0.0 collective-permute-start
  15.7 0.0 copy-done.11
  15.7 0.0 copy-done.10
  15.7 0.1 copy.32
  15.9 0.1 copy.38
  16.0 0.0 copy-done.9
  16.0 0.1 copy.37
  16.2 0.0 copy-done.3
  16.2 0.0 copy-start.4
  16.2 1.0 %copy-done.4 = bf16[2,16,64,64]{3,2,1,0:T(8,128)(2,1)S(1)} copy-done((bf16[2,16,64,64]{3,2,1,0:T(8,128)(2,1)S(1)}, bf16[2,16,64,64]{3,2,1,0:T(8,128)(2,1)}, u32[]{:S(2)}) %copy-start.4) | copy-done | bytes 262168
  17.2 0.0 copy-start.7
  17.2 0.0 copy-start.8
  17.2 0.7 mix_matrices.1
  17.9 0.1 fusion.2.refs_8_
  18.0 0.0 collective-permute-done.1
  18.0 1.1 %add.63 = f32[32,2048]{1,0:T(8,128)S(1)} add(f32[32,2048]{1,0:T(8,128)} %col_modes.1, f32[32,2048]{1,0:T(8,128)} %collective-permute-done.1) | non-fusion elementwise | flops 65536 | bytes 786432 | tf_op jit(solution)/shard_map/add | solution.py:330
  19.1 2.0 %collective-permute-start.2 = (f32[32,2048]{1,0:T(8,128)S(1)}, f32[32,2048]{1,0:T(8,128)S(1)}, u32[]{:S(2)}, u32[]{:S(2)}) collective-permute-start(f32[32,2048]{1,0:T(8,128)S(1)} %add.63), channel_id=1, source_target_pairs={{0,2},{1,3},{2,0},{3,1},{4,6},{5,7},{6,4},{7,5},{8,10},{9,11},{10,... | collective-permute-start | bytes 786440 | tf_op jit(solution)/shard_map/ppermute | solution.py:330
  21.1 0.0 collective-permute-done.3
  21.1 0.0 copy-done.7
  21.1 1.2 %add_convert_fusion.2 = bf16[32,64,128]{2,1,0:T(8,128)(2,1)S(1)} fusion(bf16[32,64,128]{2,1,0:T(8,128)(2,1)} %collective-permute-done.3, bf16[32,64,128]{2,1,0:T(8,128)(2,1)S(1)} %copy-done.7), kind=kLoop, calls=%fused_computation.4 | loop fusion | flops 1048576 | bytes 1572864 | tf_op jit(solution)/shard_map/convert_element_type | solution.py:317
  22.3 3.7 %collective-permute-start.4 = (bf16[32,64,128]{2,1,0:T(8,128)(2,1)S(1)}, bf16[32,64,128]{2,1,0:T(8,128)(2,1)}, u32[]{:S(2)}, u32[]{:S(2)}) collective-permute-start(bf16[32,64,128]{2,1,0:T(8,128)(2,1)S(1)} %add_convert_fusion.2), channel_id=1, source_target_pairs={{0,12},{12,0},{4,8},{8,4},{1,13},{13,1},{5,9},{9,5},{2,14},{14,2},... | collective-permute-start | bytes 1572872 | tf_op jit(solution)/shard_map/ppermute | solution.py:367
  26.0 1.7 %collective-permute-done.2 = f32[32,2048]{1,0:T(8,128)S(1)} collective-permute-done((f32[32,2048]{1,0:T(8,128)S(1)}, f32[32,2048]{1,0:T(8,128)S(1)}, u32[]{:S(2)}, u32[]{:S(2)}) %collective-permute-start.2) | collective-permute-done | bytes 262176 | tf_op jit(solution)/shard_map/ppermute | solution.py:330
  27.7 3.3 %collective-permute-done = bf16[32,64,128]{2,1,0:T(8,128)(2,1)} collective-permute-done((bf16[32,64,128]{2,1,0:T(8,128)(2,1)}, bf16[32,64,128]{2,1,0:T(8,128)(2,1)}, u32[]{:S(2)}, u32[]{:S(2)}) %collective-permute-start) | collective-permute-done | bytes 524320 | tf_op jit(solution)/shard_map/ppermute | solution.py:355
  31.0 0.0 copy-done.8
  31.0 2.0 %add_convert_fusion.3 = bf16[32,64,128]{2,1,0:T(8,128)(2,1)} fusion(bf16[32,64,128]{2,1,0:T(8,128)(2,1)} %collective-permute-done, bf16[32,64,128]{2,1,0:T(8,128)(2,1)S(1)} %copy-done.8), kind=kLoop, calls=%fused_computation.5 | loop fusion | flops 1048576 | bytes 1572864 | tf_op jit(solution)/shard_map/convert_element_type | solution.py:317
  33.1 0.4 reshape.205
  33.4 20.3 %collective-permute-start.5 = (bf16[32,64,128]{2,1,0:T(8,128)(2,1)}, bf16[32,64,128]{2,1,0:T(8,128)(2,1)}, u32[]{:S(2)}, u32[]{:S(2)}) collective-permute-start(bf16[32,64,128]{2,1,0:T(8,128)(2,1)} %add_convert_fusion.3), channel_id=1, source_target_pairs={{0,12},{12,0},{4,8},{8,4},{1,13},{13,1},{5,9},{9,5},{2,14},{14,2},... | collective-permute-start | bytes 1572872 | tf_op jit(solution)/shard_map/ppermute | solution.py:367
  53.7 0.4 fusion
  54.1 0.1 copy.34
  54.2 0.9 reshape.206
  55.1 0.0 copy-start.6
  55.1 2.1 %copy.35 = bf16[32,64,32]{0,1,2:T(8,128)(2,1)} copy(bf16[32,64,32]{1,0,2:T(8,128)(2,1)} %reshape.206) | data formatting | bytes 262144 | tf_op jit(solution)/shard_map/reshape | solution.py:373
  57.2 0.1 broadcast_in_dim.12
  57.3 1.5 %pad_maximum_fusion.refs_5_ = bf16[32,64,96]{2,1,0:T(8,128)(2,1)S(1)} fusion(bf16[32,64,32]{2,1,0:T(8,128)(2,1)} %bitcast.14, bf16[32,64,64]{2,1,0:T(8,128)(2,1)S(1)} %broadcast_in_dim.12), kind=kLoop, calls=%fused_computation.6 | loop fusion | flops 786432 | bytes 786432 | tf_op jit(solution)/shard_map/concatenate | solution.py:375
  58.8 0.0 collective-permute-done.4
  58.8 1.2 %add_convert_fusion.1.refs_1_.refs_2_ = bf16[32,64,128]{2,1,0:T(8,128)(2,1)S(1)} fusion(bf16[32,64,128]{2,1,0:T(8,128)(2,1)} %collective-permute-done.4, bf16[32,64,128]{2,1,0:T(8,128)(2,1)S(1)} %add_convert_fusion.2), kind=kLoop, calls=%fused_computation.3 | loop fusion | flops 1048576 | bytes 1572864 | tf_op jit(solution)/shard_map/convert_element_type | solution.py:317
  60.0 0.1 collective-permute-start.7
  60.1 0.0 copy-done.12
  60.1 0.1 broadcast_in_dim.15.refs_10_
  60.2 0.0 copy-done
  60.2 0.0 copy-done.2
  60.2 0.0 copy-done.5
  60.2 0.0 copy-done.6
  60.2 0.0 copy-done.1
  60.2 6.3 %finish.3.refs_12_ = bf16[64,32,512]{2,1,0:T(8,128)(2,1)} custom-call(s32[3]{0:T(128)S(1)} %copy-done.6, bf16[32,64,128]{2,1,0:T(8,128)(2,1)S(1)} %add_convert_fusion.1.refs_1_.refs_2_, bf16[32,64,128]{2,1,0:T(8,128)(2,1)S(1)} %add_convert_fusion.1.refs_1_.refs_2_, bf16[16,128,128]{2,1,0:T(8,128)(2,1)S(1)} %get-tuple-element.20.refs_3_, ...), custom_call_target="tpu_custom_call" | custom-call | tf_op jit(solution)/shard_map/finish/pallas_call | solution.py:293
  66.6 0.0 collective-permute-done.5
  66.6 1.4 %add_convert_fusion.refs_2_ = bf16[32,64,128]{2,1,0:T(8,128)(2,1)S(1)} fusion(bf16[32,64,128]{2,1,0:T(8,128)(2,1)} %collective-permute-done.5, bf16[32,64,128]{2,1,0:T(8,128)(2,1)} %add_convert_fusion.3), kind=kLoop, calls=%fused_computation.2 | loop fusion | flops 1048576 | bytes 1572864 | tf_op jit(solution)/shard_map/convert_element_type | solution.py:317
  67.9 4.9 %collective-permute-start.6 = (bf16[32,64,128]{2,1,0:T(8,128)(2,1)S(1)}, bf16[32,64,128]{2,1,0:T(8,128)(2,1)S(1)}, u32[]{:S(2)}, u32[]{:S(2)}) collective-permute-start(bf16[32,64,128]{2,1,0:T(8,128)(2,1)S(1)} %add_convert_fusion.refs_2_), channel_id=1, source_target_pairs={{0,4},{4,0},{8,12},{12,8},{1,5},{5,1},{9,13},{13,9},{2,6},{6,2},{1... | collective-permute-start | bytes 1572872 | tf_op jit(solution)/shard_map/ppermute | solution.py:406
  72.8 0.0 collective-permute-done.7.refs_1_
  72.8 11.9 %finish.4.refs_12_ = bf16[64,32,512]{2,1,0:T(8,128)(2,1)} custom-call(s32[3]{0:T(128)S(1)} %copy-done.6, bf16[32,64,128]{2,1,0:T(8,128)(2,1)S(1)} %collective-permute-done.7.refs_1_, bf16[32,64,128]{2,1,0:T(8,128)(2,1)S(1)} %add_convert_fusion.refs_2_, bf16[16,128,128]{2,1,0:T(8,128)(2,1)S(1)} %get-tuple-element.20.refs_3_, ...), custom_call_target="tpu_custom_call", output_to_operand_aliasing={{}: (12, {})} | custom-call | tf_op jit(solution)/shard_map/finish/pallas_call | solution.py:293
  84.7 0.0 collective-permute-done.6.refs_1_.refs_2_
  84.7 6.3 %finish.5 = bf16[64,32,512]{2,1,0:T(8,128)(2,1)} custom-call(s32[3]{0:T(128)S(1)} %copy-done.6, bf16[32,64,128]{2,1,0:T(8,128)(2,1)S(1)} %collective-permute-done.6.refs_1_.refs_2_, bf16[32,64,128]{2,1,0:T(8,128)(2,1)S(1)} %collective-permute-done.6.refs_1_.refs_2_, ...), custom_call_target="tpu_custom_call", output_to_operand_aliasing={{}: (12, {})} | custom-call | tf_op jit(solution)/shard_map/finish/pallas_call | solution.py:293
  (18 shorter events, 0.2 us)
Async XLA Ops:
  4.1 17.0 %collective-permute-start.3 = (bf16[32,64,128]{2,1,0:T(8,128)(2,1)}, bf16[32,64,128]{2,1,0:T(8,128)(2,1)}, u32[]{:S(2)}, u32[]{:S(2)}) collective-permute-start(bf16[32,64,128]{2,1,0:T(8,128)(2,1)} %get-tuple-element.19), channel_id=1, source_target_pairs={{0,4},{4,0},{8,12},{12,8},{1,5},{5,1},{9,13},{13,9},{2,6},{6,2},{1... | collective-permute-start | bytes 1572872 | tf_op jit(solution)/shard_map/ppermute | solution.py:355
  11.9 3.7 %copy-start.11 = (f32[256]{0:T(256)S(1)}, f32[256]{0:T(256)}, u32[]{:S(2)}) copy-start(f32[256]{0:T(256)} %param.16) | copy-start | bytes 3076
  11.9 3.8 %copy-start.10 = (bf16[64,64]{1,0:T(8,128)(2,1)S(1)}, bf16[64,64]{1,0:T(8,128)(2,1)}, u32[]{:S(2)}) copy-start(bf16[64,64]{1,0:T(8,128)(2,1)} %param.14) | copy-start | bytes 24580
  11.9 4.1 %copy-start.9 = (bf16[64,256]{1,0:T(8,128)(2,1)S(1)}, bf16[64,256]{1,0:T(8,128)(2,1)}, u32[]{:S(2)}) copy-start(bf16[64,256]{1,0:T(8,128)(2,1)} %param.15) | copy-start | bytes 98308
  11.9 4.2 %copy-start.3 = (bf16[2,16,64,64]{3,2,1,0:T(8,128)(2,1)S(1)}, bf16[2,16,64,64]{3,2,1,0:T(8,128)(2,1)}, u32[]{:S(2)}) copy-start(bf16[2,16,64,64]{3,2,1,0:T(8,128)(2,1)} %row_ref.1) | copy-start | bytes 786436
  11.9 6.1 %collective-permute-start.1 = (f32[32,2048]{1,0:T(8,128)}, f32[32,2048]{1,0:T(8,128)}, u32[]{:S(2)}, u32[]{:S(2)}) collective-permute-start(f32[32,2048]{1,0:T(8,128)} %col_modes.1), channel_id=1, source_target_pairs={{0,1},{1,0},{2,3},{3,2},{4,5},{5,4},{6,7},{7,6},{8,9},{9,8},{10,11... | collective-permute-start | bytes 786440 | tf_op jit(solution)/shard_map/ppermute | solution.py:330
  15.6 15.4 %collective-permute-start = (bf16[32,64,128]{2,1,0:T(8,128)(2,1)}, bf16[32,64,128]{2,1,0:T(8,128)(2,1)}, u32[]{:S(2)}, u32[]{:S(2)}) collective-permute-start(bf16[32,64,128]{2,1,0:T(8,128)(2,1)} %get-tuple-element.16), channel_id=1, source_target_pairs={{0,4},{4,0},{8,12},{12,8},{1,5},{5,1},{9,13},{13,9},{2,6},{6,2},{1... | collective-permute-start | bytes 1572872 | tf_op jit(solution)/shard_map/ppermute | solution.py:355
  16.2 1.0 %copy-start.4 = (bf16[2,16,64,64]{3,2,1,0:T(8,128)(2,1)S(1)}, bf16[2,16,64,64]{3,2,1,0:T(8,128)(2,1)}, u32[]{:S(2)}) copy-start(bf16[2,16,64,64]{3,2,1,0:T(8,128)(2,1)} %col_ref.1) | copy-start | bytes 786436
  17.2 3.9 %copy-start.7 = (bf16[32,64,128]{2,1,0:T(8,128)(2,1)S(1)}, bf16[32,64,128]{2,1,0:T(8,128)(2,1)}, u32[]{:S(2)}) copy-start(bf16[32,64,128]{2,1,0:T(8,128)(2,1)} %get-tuple-element.18) | copy-start | bytes 1572868
  17.2 13.8 %copy-start.8 = (bf16[32,64,128]{2,1,0:T(8,128)(2,1)S(1)}, bf16[32,64,128]{2,1,0:T(8,128)(2,1)}, u32[]{:S(2)}) copy-start(bf16[32,64,128]{2,1,0:T(8,128)(2,1)} %get-tuple-element.15) | copy-start | bytes 1572868
  19.1 8.6 %collective-permute-start.2 = (f32[32,2048]{1,0:T(8,128)S(1)}, f32[32,2048]{1,0:T(8,128)S(1)}, u32[]{:S(2)}, u32[]{:S(2)}) collective-permute-start(f32[32,2048]{1,0:T(8,128)S(1)} %add.63), channel_id=1, source_target_pairs={{0,2},{1,3},{2,0},{3,1},{4,6},{5,7},{6,4},{7,5},{8,10},{9,11},{10,... | collective-permute-start | bytes 786440 | tf_op jit(solution)/shard_map/ppermute | solution.py:330
  22.3 36.5 %collective-permute-start.4 = (bf16[32,64,128]{2,1,0:T(8,128)(2,1)S(1)}, bf16[32,64,128]{2,1,0:T(8,128)(2,1)}, u32[]{:S(2)}, u32[]{:S(2)}) collective-permute-start(bf16[32,64,128]{2,1,0:T(8,128)(2,1)S(1)} %add_convert_fusion.2), channel_id=1, source_target_pairs={{0,12},{12,0},{4,8},{8,4},{1,13},{13,1},{5,9},{9,5},{2,14},{14,2},... | collective-permute-start | bytes 1572872 | tf_op jit(solution)/shard_map/ppermute | solution.py:367
  33.4 33.1 %collective-permute-start.5 = (bf16[32,64,128]{2,1,0:T(8,128)(2,1)}, bf16[32,64,128]{2,1,0:T(8,128)(2,1)}, u32[]{:S(2)}, u32[]{:S(2)}) collective-permute-start(bf16[32,64,128]{2,1,0:T(8,128)(2,1)} %add_convert_fusion.3), channel_id=1, source_target_pairs={{0,12},{12,0},{4,8},{8,4},{1,13},{13,1},{5,9},{9,5},{2,14},{14,2},... | collective-permute-start | bytes 1572872 | tf_op jit(solution)/shard_map/ppermute | solution.py:367
  55.1 5.0 %copy-start.12 = (f32[64]{0:T(128)S(1)}, f32[64]{0:T(128)}, u32[]{:S(2)}) copy-start(f32[64]{0:T(128)} %param.18) | copy-start | bytes 772
  55.1 5.1 %copy-start = (bf16[64,32,512]{2,1,0:T(8,128)(2,1)S(1)}, bf16[64,32,512]{2,1,0:T(8,128)(2,1)}, u32[]{:S(2)}) copy-start(bf16[64,32,512]{2,1,0:T(8,128)(2,1)} %refs_6_.5) | copy-start | bytes 6291460
  55.1 5.1 %copy-start.2 = (bf16[256,256]{1,0:T(8,128)(2,1)S(1)}, bf16[256,256]{1,0:T(8,128)(2,1)}, u32[]{:S(2)}) copy-start(bf16[256,256]{1,0:T(8,128)(2,1)} %constant.51.clone.refs_11_) | copy-start | bytes 393220
  55.1 5.1 %copy-start.5 = (bf16[256,64]{0,1:T(8,128)(2,1)S(1)}, bf16[256,64]{0,1:T(8,128)(2,1)}, u32[]{:S(2)}) copy-start(bf16[256,64]{0,1:T(8,128)(2,1)} %param.17) | copy-start | bytes 98308
  55.1 5.1 %copy-start.6 = (s32[3]{0:T(128)S(1)}, s32[3]{0:T(128)}, u32[]{:S(2)}) copy-start(s32[3]{0:T(128)} %pad_add_fusion.place_ref.refs_0_) | copy-start | bytes 40
  57.2 3.0 %copy-start.1 = (bf16[4,512,512]{2,1,0:T(8,128)(2,1)S(1)}, bf16[4,512,512]{2,1,0:T(8,128)(2,1)}, u32[]{:S(2)}) copy-start(bf16[4,512,512]{2,1,0:T(8,128)(2,1)} %constant.52.clone.refs_4_) | copy-start | bytes 6291460
  60.0 12.8 %collective-permute-start.7 = (bf16[32,64,128]{2,1,0:T(8,128)(2,1)S(1)}, bf16[32,64,128]{2,1,0:T(8,128)(2,1)S(1)}, u32[]{:S(2)}, u32[]{:S(2)}) collective-permute-start(bf16[32,64,128]{2,1,0:T(8,128)(2,1)S(1)} %add_convert_fusion.1.refs_1_.refs_2_), channel_id=1, source_target_pairs={{0,4},{4,0},{8,12},{12,8},{1,5},{5,1},{9,13},{13,9},{2,6},{6,2},{1... | collective-permute-start | bytes 1572872 | tf_op jit(solution)/shard_map/ppermute | solution.py:406
  67.9 16.8 %collective-permute-start.6 = (bf16[32,64,128]{2,1,0:T(8,128)(2,1)S(1)}, bf16[32,64,128]{2,1,0:T(8,128)(2,1)S(1)}, u32[]{:S(2)}, u32[]{:S(2)}) collective-permute-start(bf16[32,64,128]{2,1,0:T(8,128)(2,1)S(1)} %add_convert_fusion.refs_2_), channel_id=1, source_target_pairs={{0,4},{4,0},{8,12},{12,8},{1,5},{5,1},{9,13},{13,9},{2,6},{6,2},{1... | collective-permute-start | bytes 1572872 | tf_op jit(solution)/shard_map/ppermute | solution.py:406

commit v4 on v3

--- a/solution.py
+++ b/solution.py
@@ -36,6 +36,7 @@
     phases = np.arange(mode_count)[:, None] * np.arange(period)[None, :] % period
     angles = phases.astype(np.float64) * (2.0 * math.pi / period)
     table = np.stack([np.cos(angles), -np.sin(angles)], axis=1).reshape(2 * mode_count, shares, row_count)
+    table = np.concatenate([table[:1], table[2:], table[1:2]], axis=0)
     eye = np.eye(HALF_GROUP)
     whole = np.einsum("jsx,cd->sjcdx", table, eye)
     return jnp.asarray(
@@ -107,16 +108,16 @@
                 modes = jnp.dot(table[0], block, preferred_element_type=jnp.float32)
                 parts.append(modes.reshape(-1, HALF_GROUP, LANES))
             at = slice(g * GROUP, (g + 1) * GROUP)
-            target[:, at, :] = jnp.concatenate(parts, axis=1).astype(jnp.bfloat16)
+            target[:, at, :] = jnp.concatenate(parts, axis=1)[: target.shape[0]].astype(jnp.bfloat16)
 
 
 def row_modes(place, tables, plane, mode_count, base):
     channels, row_count, _ = plane.shape
-    modes = 2 * mode_count
+    modes = 2 * mode_count - 1
     groups = channels // STEP_CHANNELS
     shape = jax.ShapeDtypeStruct((modes, channels, LANES), jnp.bfloat16)
     block = pl.BlockSpec((modes, STEP_CHANNELS, LANES), lambda g, place: (0, g, 0))
-    rows = modes * HALF_GROUP
+    rows = tables.shape[1]
 
     table_at = pl.BlockSpec((1, rows, tables.shape[2]), lambda g, place: (place[2], 0, 0))
 
@@ -189,8 +190,11 @@
 
     def mix(source):
         for k in range(mode_rows // 2):
-            pair = source[2 * k : 2 * k + 2].reshape(2 * channels, LANES)
-            mixed = jnp.dot(mix_ref[k], pair, preferred_element_type=jnp.float32)
+            if k:
+                pair = source[2 * k - 1 : 2 * k + 1].reshape(2 * channels, LANES)
+                mixed = jnp.dot(mix_ref[k], pair, preferred_element_type=jnp.float32)
+            else:
+                mixed = jnp.dot(mix_ref[0, :, :channels], source[0], preferred_element_type=jnp.float32)
             mixed = (mixed * row_scale).astype(jnp.bfloat16)
             mixed_ref[2 * k : 2 * k + 2] = mixed.reshape(2, channels, LANES)
 
@@ -255,7 +259,7 @@
     mix, inverse, local, up, down, down_bias, order = shared
     single = len(modes) == 1
     modes, more = modes[0], modes[-1]
-    mode_rows = modes.shape[0]
+    mode_rows = modes.shape[0] + 1
 
     def column(i, place):
         (base, which), (last_base, last_which) = at[0], at[-1]

time: 91.6 us -> 90.8 us (level)
  starting transfers between devices: 34 us -> 35.8 us
  waiting for transfers between devices: 5.01 us -> 3.67 us
    ppermute x2, starting transfers between devices: 4.97 us -> 7.39 us  [body(): theirs = lax.ppermute(mine, 'gx', NEAR)]
    ppermute x2, waiting for transfers between devices: 1.73 us -> 0.01 us  [sum_over_cols_axis(): lax.ppermute(value, 'gy', [(i, i ^ step) for i in range(size)])]
    concatenate x1, other arithmetic: 1.47 us -> 0.31 us  [body(): local = jnp.concatenate([skip, col_mixed], axis=2)]
    convert_element_type x4, other arithmetic: 5.87 us -> 6.95 us  [add(): return (a.astype(jnp.float32) + b.astype(jnp.float32)).astype(jnp.bfloat16)]
  transfers between devices with their start and end apart: 8 -> 8, of which waited for: 2 -> 1; matrix products, arithmetic and copies ran while one was open for 15% -> 14% of each run, Pallas kernels for 29% -> 29%
where the time goes in v4:
time: 90.8 us; the launch traced here: 90.4 us
  Pallas kernels  36 us (40%)
  starting transfers between devices  35.8 us (39%)
  other arithmetic  9.15 us (10%)
  local copies, waits for them, and re-layouts  5.01 us (6%)
  waiting for transfers between devices  3.67 us (4%)
    pallas_call x3, Pallas kernels, finish(): pl.pallas_call(kernel, out_shape=jax.ShapeDtypeStruct((channels, row_coun...  24.3 us
    ppermute x2, starting transfers between devices, body(): far = [lax.ppermute(value, 'gx', FAR) for value in half]  23.4 us
    ppermute x2, starting transfers between devices, body(): theirs = lax.ppermute(mine, 'gx', NEAR)  7.39 us
    pallas_call x2, Pallas kernels, row_modes(): pl.pallas_call(row_modes_kernel, out_shape=(shape, shape), grid_spec=pltp...  7.12 us
    convert_element_type x4, other arithmetic, add(): return (a.astype(jnp.float32) + b.astype(jnp.float32)).astype(jnp.bfloat16)  6.95 us
    pallas_call x1, Pallas kernels, col_modes(): pl.pallas_call(col_modes_kernel, out_shape=jax.ShapeDtypeStruct((modes, c...  3.94 us
    ppermute x2, waiting for transfers between devices, body(): near = [lax.ppermute(send, 'gx', NEAR) for send, _ in partial]  3.66 us
    ppermute x2, starting transfers between devices, body(): near = [lax.ppermute(send, 'gx', NEAR) for send, _ in partial]  3.06 us
  transfers between devices with their start and end apart: 8, of which 1 were waited for; matrix products, arithmetic and copies ran while one was open for 14% of the time, Pallas kernels for 29%

profile of v4, /device:TPU:0, one launch (start us, length us, event | category | flops | bytes accessed | tf_op | source)
XLA Modules:
  0.0 90.4 jit_solution(14335517620009291951)
XLA Ops:
  0.0 0.6 pad_add_fusion.place_ref.refs_0_
  0.6 3.5 %row_modes.3 = (bf16[31,64,128]{2,1,0:T(8,128)(2,1)}, bf16[31,64,128]{2,1,0:T(8,128)(2,1)}) custom-call(s32[3]{0:T(128)} %pad_add_fusion.place_ref.refs_0_, bf16[4,256,256]{2,1,0:T(8,128)(2,1)} %constant.50.clone.table, bf16[64,32,512]{2,1,0:T(8,128)(2,1)} %refs_6_.5, bf16[64,32,512]{2,1,0:T(8,128)(2,1)} %refs_6_.5), custom_call_target="tpu_custom_call" | custom-call | tf_op jit(solution)/shard_map/row_modes/pallas_call | solution.py:130
  4.1 3.0 %collective-permute-start.3 = (bf16[31,64,128]{2,1,0:T(8,128)(2,1)}, bf16[31,64,128]{2,1,0:T(8,128)(2,1)}, u32[]{:S(2)}, u32[]{:S(2)}) collective-permute-start(bf16[31,64,128]{2,1,0:T(8,128)(2,1)} %get-tuple-element.19), channel_id=1, source_target_pairs={{0,4},{4,0},{8,12},{12,8},{1,5},{5,1},{9,13},{13,9},{2,6},{6,2},{1... | collective-permute-start | bytes 1523720 | tf_op jit(solution)/shard_map/ppermute | solution.py:359
  7.1 0.2 multiply_convert_fusion.1
  7.4 0.6 convert_element_type.78.table_ref
  8.0 3.9 %col_modes.1 = f32[32,2048]{1,0:T(8,128)} custom-call(bf16[32,512]{1,0:T(8,128)(2,1)} %convert_element_type.78.table_ref, bf16[64,32,512]{2,1,0:T(8,128)(2,1)} %refs_6_.5), custom_call_target="tpu_custom_call" | custom-call | tf_op jit(solution)/shard_map/col_modes/pallas_call | solution.py:155
  11.9 0.0 copy-start.12
  11.9 0.0 copy-start.11
  11.9 0.0 copy-start.3
  12.0 0.0 copy-start.7
  12.0 0.1 collective-permute-start.1
  12.0 3.6 %row_modes.2 = (bf16[31,64,128]{2,1,0:T(8,128)(2,1)}, bf16[31,64,128]{2,1,0:T(8,128)(2,1)}) custom-call(s32[3]{0:T(128)} %pad_add_fusion.place_ref.refs_0_, bf16[4,256,256]{2,1,0:T(8,128)(2,1)} %constant.50.clone.table, bf16[64,32,512]{2,1,0:T(8,128)(2,1)} %refs_6_.5, bf16[64,32,512]{2,1,0:T(8,128)(2,1)} %refs_6_.5), custom_call_target="tpu_custom_call" | custom-call | tf_op jit(solution)/shard_map/row_modes/pallas_call | solution.py:130
  15.7 0.0 collective-permute-start
  15.7 0.0 copy-done.12
  15.7 0.0 copy-done.11
  15.7 0.1 copy.32
  15.9 0.1 copy.38
  16.1 0.0 copy-done.10
  16.1 0.1 copy.37
  16.2 0.0 copy-done.3
  16.2 0.0 copy-start.4
  16.2 1.0 %copy-done.4 = bf16[2,16,64,64]{3,2,1,0:T(8,128)(2,1)S(1)} copy-done((bf16[2,16,64,64]{3,2,1,0:T(8,128)(2,1)S(1)}, bf16[2,16,64,64]{3,2,1,0:T(8,128)(2,1)}, u32[]{:S(2)}) %copy-start.4) | copy-done | bytes 262168
  17.3 0.7 mix_matrices.1
  18.0 0.1 fusion.2.refs_8_
  18.0 0.0 collective-permute-done.1
  18.1 0.0 copy-done.7
  18.1 1.0 %add.63 = f32[32,2048]{1,0:T(8,128)S(1)} add(f32[32,2048]{1,0:T(8,128)S(1)} %copy-done.7, f32[32,2048]{1,0:T(8,128)} %collective-permute-done.1) | non-fusion elementwise | flops 65536 | bytes 786432 | tf_op jit(solution)/shard_map/add | solution.py:334
  19.1 2.0 %collective-permute-start.2 = (f32[32,2048]{1,0:T(8,128)S(1)}, f32[32,2048]{1,0:T(8,128)S(1)}, u32[]{:S(2)}, u32[]{:S(2)}) collective-permute-start(f32[32,2048]{1,0:T(8,128)S(1)} %add.63), channel_id=1, source_target_pairs={{0,2},{1,3},{2,0},{3,1},{4,6},{5,7},{6,4},{7,5},{8,10},{9,11},{10,... | collective-permute-start | bytes 786440 | tf_op jit(solution)/shard_map/ppermute | solution.py:334
  21.0 0.0 collective-permute-done.3
  21.0 0.0 copy-done.8
  21.0 2.0 %add_convert_fusion.2 = bf16[31,64,128]{2,1,0:T(8,128)(2,1)} fusion(bf16[31,64,128]{2,1,0:T(8,128)(2,1)} %collective-permute-done.3, bf16[31,64,128]{2,1,0:T(8,128)(2,1)S(1)} %copy-done.8), kind=kLoop, calls=%fused_computation.4 | loop fusion | flops 1015808 | bytes 1523712 | tf_op jit(solution)/shard_map/convert_element_type | solution.py:321
  23.1 3.6 %collective-permute-start.4 = (bf16[31,64,128]{2,1,0:T(8,128)(2,1)}, bf16[31,64,128]{2,1,0:T(8,128)(2,1)}, u32[]{:S(2)}, u32[]{:S(2)}) collective-permute-start(bf16[31,64,128]{2,1,0:T(8,128)(2,1)} %add_convert_fusion.2), channel_id=1, source_target_pairs={{0,12},{12,0},{4,8},{8,4},{1,13},{13,1},{5,9},{9,5},{2,14},{14,2},... | collective-permute-start | bytes 1523720 | tf_op jit(solution)/shard_map/ppermute | solution.py:371
  26.7 3.7 %collective-permute-done = bf16[31,64,128]{2,1,0:T(8,128)(2,1)} collective-permute-done((bf16[31,64,128]{2,1,0:T(8,128)(2,1)}, bf16[31,64,128]{2,1,0:T(8,128)(2,1)}, u32[]{:S(2)}, u32[]{:S(2)}) %collective-permute-start) | collective-permute-done | bytes 507936 | tf_op jit(solution)/shard_map/ppermute | solution.py:359
  30.3 0.0 copy-done.9
  30.3 2.0 %add_convert_fusion.3 = bf16[31,64,128]{2,1,0:T(8,128)(2,1)} fusion(bf16[31,64,128]{2,1,0:T(8,128)(2,1)} %collective-permute-done, bf16[31,64,128]{2,1,0:T(8,128)(2,1)S(1)} %copy-done.9), kind=kLoop, calls=%fused_computation.5 | loop fusion | flops 1015808 | bytes 1523712 | tf_op jit(solution)/shard_map/convert_element_type | solution.py:321
  32.3 0.0 collective-permute-done.2
  32.4 0.4 reshape.205
  32.7 19.8 %collective-permute-start.5 = (bf16[31,64,128]{2,1,0:T(8,128)(2,1)}, bf16[31,64,128]{2,1,0:T(8,128)(2,1)}, u32[]{:S(2)}, u32[]{:S(2)}) collective-permute-start(bf16[31,64,128]{2,1,0:T(8,128)(2,1)} %add_convert_fusion.3), channel_id=1, source_target_pairs={{0,12},{12,0},{4,8},{8,4},{1,13},{13,1},{5,9},{9,5},{2,14},{14,2},... | collective-permute-start | bytes 1523720 | tf_op jit(solution)/shard_map/ppermute | solution.py:371
  52.5 0.4 fusion
  52.9 0.1 copy.34
  53.0 0.8 reshape.206
  53.8 0.0 copy-start.6
  53.8 1.4 %copy.35 = bf16[32,64,32]{0,1,2:T(8,128)(2,1)S(1)} copy(bf16[32,64,32]{1,0,2:T(8,128)(2,1)} %reshape.206) | data formatting | bytes 262144 | tf_op jit(solution)/shard_map/reshape | solution.py:377
  55.2 0.0 copy-start.1
  55.2 0.1 broadcast_in_dim.12
  55.3 0.3 pad_maximum_fusion.refs_5_
  55.7 0.0 collective-permute-done.4
  55.7 1.5 %add_convert_fusion.1.refs_1_.refs_2_ = bf16[31,64,128]{2,1,0:T(8,128)(2,1)S(1)} fusion(bf16[31,64,128]{2,1,0:T(8,128)(2,1)} %collective-permute-done.4, bf16[31,64,128]{2,1,0:T(8,128)(2,1)} %add_convert_fusion.2), kind=kLoop, calls=%fused_computation.3 | loop fusion | flops 1015808 | bytes 1523712 | tf_op jit(solution)/shard_map/convert_element_type | solution.py:321
  57.2 4.4 %collective-permute-start.7 = (bf16[31,64,128]{2,1,0:T(8,128)(2,1)S(1)}, bf16[31,64,128]{2,1,0:T(8,128)(2,1)S(1)}, u32[]{:S(2)}, u32[]{:S(2)}) collective-permute-start(bf16[31,64,128]{2,1,0:T(8,128)(2,1)S(1)} %add_convert_fusion.1.refs_1_.refs_2_), channel_id=1, source_target_pairs={{0,4},{4,0},{8,12},{12,8},{1,5},{5,1},{9,13},{13,9},{2,6},{6,2},{1... | collective-permute-start | bytes 1523720 | tf_op jit(solution)/shard_map/ppermute | solution.py:410
  61.7 0.0 copy-done.13
  61.7 0.1 broadcast_in_dim.15.refs_10_
  61.7 0.0 copy-done
  61.7 0.0 copy-done.2
  61.7 0.0 copy-done.5
  61.8 0.0 copy-done.6
  61.8 0.0 copy-done.1
  61.8 6.2 %finish.3.refs_12_ = bf16[64,32,512]{2,1,0:T(8,128)(2,1)} custom-call(s32[3]{0:T(128)S(1)} %copy-done.6, bf16[31,64,128]{2,1,0:T(8,128)(2,1)S(1)} %add_convert_fusion.1.refs_1_.refs_2_, bf16[31,64,128]{2,1,0:T(8,128)(2,1)S(1)} %add_convert_fusion.1.refs_1_.refs_2_, bf16[16,128,128]{2,1,0:T(8,128)(2,1)S(1)} %get-tuple-element.20.refs_3_, ...), custom_call_target="tpu_custom_call" | custom-call | tf_op jit(solution)/shard_map/finish/pallas_call | solution.py:297
  68.0 0.0 collective-permute-done.5
  68.0 1.4 %add_convert_fusion.refs_2_ = bf16[31,64,128]{2,1,0:T(8,128)(2,1)S(1)} fusion(bf16[31,64,128]{2,1,0:T(8,128)(2,1)} %collective-permute-done.5, bf16[31,64,128]{2,1,0:T(8,128)(2,1)} %add_convert_fusion.3), kind=kLoop, calls=%fused_computation.2 | loop fusion | flops 1015808 | bytes 1523712 | tf_op jit(solution)/shard_map/convert_element_type | solution.py:321
  69.4 2.9 %collective-permute-start.6 = (bf16[31,64,128]{2,1,0:T(8,128)(2,1)S(1)}, bf16[31,64,128]{2,1,0:T(8,128)(2,1)S(1)}, u32[]{:S(2)}, u32[]{:S(2)}) collective-permute-start(bf16[31,64,128]{2,1,0:T(8,128)(2,1)S(1)} %add_convert_fusion.refs_2_), channel_id=1, source_target_pairs={{0,4},{4,0},{8,12},{12,8},{1,5},{5,1},{9,13},{13,9},{2,6},{6,2},{1... | collective-permute-start | bytes 1523720 | tf_op jit(solution)/shard_map/ppermute | solution.py:410
  72.3 0.0 collective-permute-done.7.refs_1_
  72.3 11.8 %finish.4.refs_12_ = bf16[64,32,512]{2,1,0:T(8,128)(2,1)} custom-call(s32[3]{0:T(128)S(1)} %copy-done.6, bf16[31,64,128]{2,1,0:T(8,128)(2,1)S(1)} %collective-permute-done.7.refs_1_, bf16[31,64,128]{2,1,0:T(8,128)(2,1)S(1)} %add_convert_fusion.refs_2_, bf16[16,128,128]{2,1,0:T(8,128)(2,1)S(1)} %get-tuple-element.20.refs_3_, ...), custom_call_target="tpu_custom_call", output_to_operand_aliasing={{}: (12, {})} | custom-call | tf_op jit(solution)/shard_map/finish/pallas_call | solution.py:297
  84.1 0.0 collective-permute-done.6.refs_1_.refs_2_
  84.1 6.2 %finish.5 = bf16[64,32,512]{2,1,0:T(8,128)(2,1)} custom-call(s32[3]{0:T(128)S(1)} %copy-done.6, bf16[31,64,128]{2,1,0:T(8,128)(2,1)S(1)} %collective-permute-done.6.refs_1_.refs_2_, bf16[31,64,128]{2,1,0:T(8,128)(2,1)S(1)} %collective-permute-done.6.refs_1_.refs_2_, ...), custom_call_target="tpu_custom_call", output_to_operand_aliasing={{}: (12, {})} | custom-call | tf_op jit(solution)/shard_map/finish/pallas_call | solution.py:297
  (20 shorter events, 0.2 us)
Async XLA Ops:
  4.1 16.9 %collective-permute-start.3 = (bf16[31,64,128]{2,1,0:T(8,128)(2,1)}, bf16[31,64,128]{2,1,0:T(8,128)(2,1)}, u32[]{:S(2)}, u32[]{:S(2)}) collective-permute-start(bf16[31,64,128]{2,1,0:T(8,128)(2,1)} %get-tuple-element.19), channel_id=1, source_target_pairs={{0,4},{4,0},{8,12},{12,8},{1,5},{5,1},{9,13},{13,9},{2,6},{6,2},{1... | collective-permute-start | bytes 1523720 | tf_op jit(solution)/shard_map/ppermute | solution.py:359
  11.9 3.8 %copy-start.12 = (f32[256]{0:T(256)S(1)}, f32[256]{0:T(256)}, u32[]{:S(2)}) copy-start(f32[256]{0:T(256)} %param.16) | copy-start | bytes 3076
  11.9 3.8 %copy-start.11 = (bf16[64,64]{1,0:T(8,128)(2,1)S(1)}, bf16[64,64]{1,0:T(8,128)(2,1)}, u32[]{:S(2)}) copy-start(bf16[64,64]{1,0:T(8,128)(2,1)} %param.14) | copy-start | bytes 24580
  11.9 4.1 %copy-start.10 = (bf16[64,256]{1,0:T(8,128)(2,1)S(1)}, bf16[64,256]{1,0:T(8,128)(2,1)}, u32[]{:S(2)}) copy-start(bf16[64,256]{1,0:T(8,128)(2,1)} %param.15) | copy-start | bytes 98308
  11.9 4.3 %copy-start.3 = (bf16[2,16,64,64]{3,2,1,0:T(8,128)(2,1)S(1)}, bf16[2,16,64,64]{3,2,1,0:T(8,128)(2,1)}, u32[]{:S(2)}) copy-start(bf16[2,16,64,64]{3,2,1,0:T(8,128)(2,1)} %row_ref.1) | copy-start | bytes 786436
  12.0 6.1 %copy-start.7 = (f32[32,2048]{1,0:T(8,128)S(1)}, f32[32,2048]{1,0:T(8,128)}, u32[]{:S(2)}) copy-start(f32[32,2048]{1,0:T(8,128)} %col_modes.1) | copy-start | bytes 786436
  12.0 6.1 %collective-permute-start.1 = (f32[32,2048]{1,0:T(8,128)}, f32[32,2048]{1,0:T(8,128)}, u32[]{:S(2)}, u32[]{:S(2)}) collective-permute-start(f32[32,2048]{1,0:T(8,128)} %col_modes.1), channel_id=1, source_target_pairs={{0,1},{1,0},{2,3},{3,2},{4,5},{5,4},{6,7},{7,6},{8,9},{9,8},{10,11... | collective-permute-start | bytes 786440 | tf_op jit(solution)/shard_map/ppermute | solution.py:334
  15.7 14.6 %collective-permute-start = (bf16[31,64,128]{2,1,0:T(8,128)(2,1)}, bf16[31,64,128]{2,1,0:T(8,128)(2,1)}, u32[]{:S(2)}, u32[]{:S(2)}) collective-permute-start(bf16[31,64,128]{2,1,0:T(8,128)(2,1)} %get-tuple-element.16), channel_id=1, source_target_pairs={{0,4},{4,0},{8,12},{12,8},{1,5},{5,1},{9,13},{13,9},{2,6},{6,2},{1... | collective-permute-start | bytes 1523720 | tf_op jit(solution)/shard_map/ppermute | solution.py:359
  16.2 1.0 %copy-start.4 = (bf16[2,16,64,64]{3,2,1,0:T(8,128)(2,1)S(1)}, bf16[2,16,64,64]{3,2,1,0:T(8,128)(2,1)}, u32[]{:S(2)}) copy-start(bf16[2,16,64,64]{3,2,1,0:T(8,128)(2,1)} %col_ref.1) | copy-start | bytes 786436
  17.3 3.8 %copy-start.8 = (bf16[31,64,128]{2,1,0:T(8,128)(2,1)S(1)}, bf16[31,64,128]{2,1,0:T(8,128)(2,1)}, u32[]{:S(2)}) copy-start(bf16[31,64,128]{2,1,0:T(8,128)(2,1)} %get-tuple-element.18) | copy-start | bytes 1523716
  17.3 13.1 %copy-start.9 = (bf16[31,64,128]{2,1,0:T(8,128)(2,1)S(1)}, bf16[31,64,128]{2,1,0:T(8,128)(2,1)}, u32[]{:S(2)}) copy-start(bf16[31,64,128]{2,1,0:T(8,128)(2,1)} %get-tuple-element.15) | copy-start | bytes 1523716
  19.1 13.3 %collective-permute-start.2 = (f32[32,2048]{1,0:T(8,128)S(1)}, f32[32,2048]{1,0:T(8,128)S(1)}, u32[]{:S(2)}, u32[]{:S(2)}) collective-permute-start(f32[32,2048]{1,0:T(8,128)S(1)} %add.63), channel_id=1, source_target_pairs={{0,2},{1,3},{2,0},{3,1},{4,6},{5,7},{6,4},{7,5},{8,10},{9,11},{10,... | collective-permute-start | bytes 786440 | tf_op jit(solution)/shard_map/ppermute | solution.py:334
  23.1 32.6 %collective-permute-start.4 = (bf16[31,64,128]{2,1,0:T(8,128)(2,1)}, bf16[31,64,128]{2,1,0:T(8,128)(2,1)}, u32[]{:S(2)}, u32[]{:S(2)}) collective-permute-start(bf16[31,64,128]{2,1,0:T(8,128)(2,1)} %add_convert_fusion.2), channel_id=1, source_target_pairs={{0,12},{12,0},{4,8},{8,4},{1,13},{13,1},{5,9},{9,5},{2,14},{14,2},... | collective-permute-start | bytes 1523720 | tf_op jit(solution)/shard_map/ppermute | solution.py:371
  32.7 35.2 %collective-permute-start.5 = (bf16[31,64,128]{2,1,0:T(8,128)(2,1)}, bf16[31,64,128]{2,1,0:T(8,128)(2,1)}, u32[]{:S(2)}, u32[]{:S(2)}) collective-permute-start(bf16[31,64,128]{2,1,0:T(8,128)(2,1)} %add_convert_fusion.3), channel_id=1, source_target_pairs={{0,12},{12,0},{4,8},{8,4},{1,13},{13,1},{5,9},{9,5},{2,14},{14,2},... | collective-permute-start | bytes 1523720 | tf_op jit(solution)/shard_map/ppermute | solution.py:371
  53.8 7.8 %copy-start.13 = (f32[64]{0:T(128)S(1)}, f32[64]{0:T(128)}, u32[]{:S(2)}) copy-start(f32[64]{0:T(128)} %param.18) | copy-start | bytes 772
  53.8 7.9 %copy-start = (bf16[64,32,512]{2,1,0:T(8,128)(2,1)S(1)}, bf16[64,32,512]{2,1,0:T(8,128)(2,1)}, u32[]{:S(2)}) copy-start(bf16[64,32,512]{2,1,0:T(8,128)(2,1)} %refs_6_.5) | copy-start | bytes 6291460
  53.8 7.9 %copy-start.2 = (bf16[256,256]{1,0:T(8,128)(2,1)S(1)}, bf16[256,256]{1,0:T(8,128)(2,1)}, u32[]{:S(2)}) copy-start(bf16[256,256]{1,0:T(8,128)(2,1)} %constant.51.clone.refs_11_) | copy-start | bytes 393220
  53.8 7.9 %copy-start.5 = (bf16[256,64]{0,1:T(8,128)(2,1)S(1)}, bf16[256,64]{0,1:T(8,128)(2,1)}, u32[]{:S(2)}) copy-start(bf16[256,64]{0,1:T(8,128)(2,1)} %param.17) | copy-start | bytes 98308
  53.8 7.9 %copy-start.6 = (s32[3]{0:T(128)S(1)}, s32[3]{0:T(128)}, u32[]{:S(2)}) copy-start(s32[3]{0:T(128)} %pad_add_fusion.place_ref.refs_0_) | copy-start | bytes 40
  55.2 6.5 %copy-start.1 = (bf16[4,512,512]{2,1,0:T(8,128)(2,1)S(1)}, bf16[4,512,512]{2,1,0:T(8,128)(2,1)}, u32[]{:S(2)}) copy-start(bf16[4,512,512]{2,1,0:T(8,128)(2,1)} %constant.52.clone.refs_4_) | copy-start | bytes 6291460
  57.2 15.1 %collective-permute-start.7 = (bf16[31,64,128]{2,1,0:T(8,128)(2,1)S(1)}, bf16[31,64,128]{2,1,0:T(8,128)(2,1)S(1)}, u32[]{:S(2)}, u32[]{:S(2)}) collective-permute-start(bf16[31,64,128]{2,1,0:T(8,128)(2,1)S(1)} %add_convert_fusion.1.refs_1_.refs_2_), channel_id=1, source_target_pairs={{0,4},{4,0},{8,12},{12,8},{1,5},{5,1},{9,13},{13,9},{2,6},{6,2},{1... | collective-permute-start | bytes 1523720 | tf_op jit(solution)/shard_map/ppermute | solution.py:410
  69.4 14.8 %collective-permute-start.6 = (bf16[31,64,128]{2,1,0:T(8,128)(2,1)S(1)}, bf16[31,64,128]{2,1,0:T(8,128)(2,1)S(1)}, u32[]{:S(2)}, u32[]{:S(2)}) collective-permute-start(bf16[31,64,128]{2,1,0:T(8,128)(2,1)S(1)} %add_convert_fusion.refs_2_), channel_id=1, source_target_pairs={{0,4},{4,0},{8,12},{12,8},{1,5},{5,1},{9,13},{13,9},{2,6},{6,2},{1... | collective-permute-start | bytes 1523720 | tf_op jit(solution)/shard_map/ppermute | solution.py:410

commit v5 on v4

--- a/solution.py
+++ b/solution.py
@@ -24,7 +24,7 @@
 
 def gelu(v):
     t = jnp.abs(v)
-    s = 1.0 / (1.0 + TAIL * t)
+    s = pl.reciprocal(1.0 + TAIL * t, approx=True)
     poly = COEFFS[-1]
     for c in COEFFS[-2::-1]:
         poly = poly * s + c

time: 90.8 us -> 90.8 us (level)
  no operation moved by 1% of the time
where the time goes in v5:
time: 90.8 us; the launch traced here: 90.4 us
  Pallas kernels  36 us (40%)
  starting transfers between devices  35.8 us (39%)
  other arithmetic  9.15 us (10%)
  local copies, waits for them, and re-layouts  5.01 us (6%)
  waiting for transfers between devices  3.67 us (4%)
    pallas_call x3, Pallas kernels, finish(): pl.pallas_call(kernel, out_shape=jax.ShapeDtypeStruct((channels, row_coun...  24.3 us
    ppermute x2, starting transfers between devices, body(): far = [lax.ppermute(value, 'gx', FAR) for value in half]  23.4 us
    ppermute x2, starting transfers between devices, body(): theirs = lax.ppermute(mine, 'gx', NEAR)  7.39 us
    pallas_call x2, Pallas kernels, row_modes(): pl.pallas_call(row_modes_kernel, out_shape=(shape, shape), grid_spec=pltp...  7.12 us
    convert_element_type x4, other arithmetic, add(): return (a.astype(jnp.float32) + b.astype(jnp.float32)).astype(jnp.bfloat16)  6.95 us
    pallas_call x1, Pallas kernels, col_modes(): pl.pallas_call(col_modes_kernel, out_shape=jax.ShapeDtypeStruct((modes, c...  3.94 us
    ppermute x2, waiting for transfers between devices, body(): near = [lax.ppermute(send, 'gx', NEAR) for send, _ in partial]  3.66 us
    ppermute x2, starting transfers between devices, body(): near = [lax.ppermute(send, 'gx', NEAR) for send, _ in partial]  3.06 us
  transfers between devices with their start and end apart: 8, of which 1 were waited for; matrix products, arithmetic and copies ran while one was open for 14% of the time, Pallas kernels for 29%

profile of v5, /device:TPU:0, one launch (start us, length us, event | category | flops | bytes accessed | tf_op | source)
XLA Modules:
  0.0 90.4 jit_solution(14335517620009291951)
XLA Ops:
  0.0 0.6 pad_add_fusion.place_ref.refs_0_
  0.6 3.5 %row_modes.3 = (bf16[31,64,128]{2,1,0:T(8,128)(2,1)}, bf16[31,64,128]{2,1,0:T(8,128)(2,1)}) custom-call(s32[3]{0:T(128)} %pad_add_fusion.place_ref.refs_0_, bf16[4,256,256]{2,1,0:T(8,128)(2,1)} %constant.50.clone.table, bf16[64,32,512]{2,1,0:T(8,128)(2,1)} %refs_6_.5, bf16[64,32,512]{2,1,0:T(8,128)(2,1)} %refs_6_.5), custom_call_target="tpu_custom_call" | custom-call | tf_op jit(solution)/shard_map/row_modes/pallas_call | solution.py:130
  4.1 3.0 %collective-permute-start.3 = (bf16[31,64,128]{2,1,0:T(8,128)(2,1)}, bf16[31,64,128]{2,1,0:T(8,128)(2,1)}, u32[]{:S(2)}, u32[]{:S(2)}) collective-permute-start(bf16[31,64,128]{2,1,0:T(8,128)(2,1)} %get-tuple-element.19), channel_id=1, source_target_pairs={{0,4},{4,0},{8,12},{12,8},{1,5},{5,1},{9,13},{13,9},{2,6},{6,2},{1... | collective-permute-start | bytes 1523720 | tf_op jit(solution)/shard_map/ppermute | solution.py:359
  7.1 0.2 multiply_convert_fusion.1
  7.4 0.6 convert_element_type.78.table_ref
  8.0 3.9 %col_modes.1 = f32[32,2048]{1,0:T(8,128)} custom-call(bf16[32,512]{1,0:T(8,128)(2,1)} %convert_element_type.78.table_ref, bf16[64,32,512]{2,1,0:T(8,128)(2,1)} %refs_6_.5), custom_call_target="tpu_custom_call" | custom-call | tf_op jit(solution)/shard_map/col_modes/pallas_call | solution.py:155
  11.9 0.0 copy-start.12
  11.9 0.0 copy-start.11
  11.9 0.0 copy-start.3
  12.0 0.0 copy-start.7
  12.0 0.1 collective-permute-start.1
  12.0 3.6 %row_modes.2 = (bf16[31,64,128]{2,1,0:T(8,128)(2,1)}, bf16[31,64,128]{2,1,0:T(8,128)(2,1)}) custom-call(s32[3]{0:T(128)} %pad_add_fusion.place_ref.refs_0_, bf16[4,256,256]{2,1,0:T(8,128)(2,1)} %constant.50.clone.table, bf16[64,32,512]{2,1,0:T(8,128)(2,1)} %refs_6_.5, bf16[64,32,512]{2,1,0:T(8,128)(2,1)} %refs_6_.5), custom_call_target="tpu_custom_call" | custom-call | tf_op jit(solution)/shard_map/row_modes/pallas_call | solution.py:130
  15.7 0.0 collective-permute-start
  15.7 0.0 copy-done.12
  15.7 0.0 copy-done.11
  15.7 0.1 copy.32
  15.9 0.1 copy.38
  16.1 0.0 copy-done.10
  16.1 0.1 copy.37
  16.2 0.0 copy-done.3
  16.2 0.0 copy-start.4
  16.2 1.0 %copy-done.4 = bf16[2,16,64,64]{3,2,1,0:T(8,128)(2,1)S(1)} copy-done((bf16[2,16,64,64]{3,2,1,0:T(8,128)(2,1)S(1)}, bf16[2,16,64,64]{3,2,1,0:T(8,128)(2,1)}, u32[]{:S(2)}) %copy-start.4) | copy-done | bytes 262168
  17.3 0.7 mix_matrices.1
  18.0 0.1 fusion.2.refs_8_
  18.0 0.0 collective-permute-done.1
  18.1 0.0 copy-done.7
  18.1 1.0 %add.63 = f32[32,2048]{1,0:T(8,128)S(1)} add(f32[32,2048]{1,0:T(8,128)S(1)} %copy-done.7, f32[32,2048]{1,0:T(8,128)} %collective-permute-done.1) | non-fusion elementwise | flops 65536 | bytes 786432 | tf_op jit(solution)/shard_map/add | solution.py:334
  19.1 2.0 %collective-permute-start.2 = (f32[32,2048]{1,0:T(8,128)S(1)}, f32[32,2048]{1,0:T(8,128)S(1)}, u32[]{:S(2)}, u32[]{:S(2)}) collective-permute-start(f32[32,2048]{1,0:T(8,128)S(1)} %add.63), channel_id=1, source_target_pairs={{0,2},{1,3},{2,0},{3,1},{4,6},{5,7},{6,4},{7,5},{8,10},{9,11},{10,... | collective-permute-start | bytes 786440 | tf_op jit(solution)/shard_map/ppermute | solution.py:334
  21.0 0.0 collective-permute-done.3
  21.0 0.0 copy-done.8
  21.0 2.0 %add_convert_fusion.2 = bf16[31,64,128]{2,1,0:T(8,128)(2,1)} fusion(bf16[31,64,128]{2,1,0:T(8,128)(2,1)} %collective-permute-done.3, bf16[31,64,128]{2,1,0:T(8,128)(2,1)S(1)} %copy-done.8), kind=kLoop, calls=%fused_computation.4 | loop fusion | flops 1015808 | bytes 1523712 | tf_op jit(solution)/shard_map/convert_element_type | solution.py:321
  23.1 3.6 %collective-permute-start.4 = (bf16[31,64,128]{2,1,0:T(8,128)(2,1)}, bf16[31,64,128]{2,1,0:T(8,128)(2,1)}, u32[]{:S(2)}, u32[]{:S(2)}) collective-permute-start(bf16[31,64,128]{2,1,0:T(8,128)(2,1)} %add_convert_fusion.2), channel_id=1, source_target_pairs={{0,12},{12,0},{4,8},{8,4},{1,13},{13,1},{5,9},{9,5},{2,14},{14,2},... | collective-permute-start | bytes 1523720 | tf_op jit(solution)/shard_map/ppermute | solution.py:371
  26.7 3.7 %collective-permute-done = bf16[31,64,128]{2,1,0:T(8,128)(2,1)} collective-permute-done((bf16[31,64,128]{2,1,0:T(8,128)(2,1)}, bf16[31,64,128]{2,1,0:T(8,128)(2,1)}, u32[]{:S(2)}, u32[]{:S(2)}) %collective-permute-start) | collective-permute-done | bytes 507936 | tf_op jit(solution)/shard_map/ppermute | solution.py:359
  30.3 0.0 copy-done.9
  30.3 2.0 %add_convert_fusion.3 = bf16[31,64,128]{2,1,0:T(8,128)(2,1)} fusion(bf16[31,64,128]{2,1,0:T(8,128)(2,1)} %collective-permute-done, bf16[31,64,128]{2,1,0:T(8,128)(2,1)S(1)} %copy-done.9), kind=kLoop, calls=%fused_computation.5 | loop fusion | flops 1015808 | bytes 1523712 | tf_op jit(solution)/shard_map/convert_element_type | solution.py:321
  32.3 0.0 collective-permute-done.2
  32.4 0.4 reshape.205
  32.7 19.8 %collective-permute-start.5 = (bf16[31,64,128]{2,1,0:T(8,128)(2,1)}, bf16[31,64,128]{2,1,0:T(8,128)(2,1)}, u32[]{:S(2)}, u32[]{:S(2)}) collective-permute-start(bf16[31,64,128]{2,1,0:T(8,128)(2,1)} %add_convert_fusion.3), channel_id=1, source_target_pairs={{0,12},{12,0},{4,8},{8,4},{1,13},{13,1},{5,9},{9,5},{2,14},{14,2},... | collective-permute-start | bytes 1523720 | tf_op jit(solution)/shard_map/ppermute | solution.py:371
  52.5 0.4 fusion
  52.9 0.1 copy.34
  53.0 0.8 reshape.206
  53.8 0.0 copy-start.6
  53.8 1.4 %copy.35 = bf16[32,64,32]{0,1,2:T(8,128)(2,1)S(1)} copy(bf16[32,64,32]{1,0,2:T(8,128)(2,1)} %reshape.206) | data formatting | bytes 262144 | tf_op jit(solution)/shard_map/reshape | solution.py:377
  55.2 0.0 copy-start.1
  55.2 0.1 broadcast_in_dim.12
  55.3 0.3 pad_maximum_fusion.refs_5_
  55.7 0.0 collective-permute-done.4
  55.7 1.5 %add_convert_fusion.1.refs_1_.refs_2_ = bf16[31,64,128]{2,1,0:T(8,128)(2,1)S(1)} fusion(bf16[31,64,128]{2,1,0:T(8,128)(2,1)} %collective-permute-done.4, bf16[31,64,128]{2,1,0:T(8,128)(2,1)} %add_convert_fusion.2), kind=kLoop, calls=%fused_computation.3 | loop fusion | flops 1015808 | bytes 1523712 | tf_op jit(solution)/shard_map/convert_element_type | solution.py:321
  57.2 4.4 %collective-permute-start.7 = (bf16[31,64,128]{2,1,0:T(8,128)(2,1)S(1)}, bf16[31,64,128]{2,1,0:T(8,128)(2,1)S(1)}, u32[]{:S(2)}, u32[]{:S(2)}) collective-permute-start(bf16[31,64,128]{2,1,0:T(8,128)(2,1)S(1)} %add_convert_fusion.1.refs_1_.refs_2_), channel_id=1, source_target_pairs={{0,4},{4,0},{8,12},{12,8},{1,5},{5,1},{9,13},{13,9},{2,6},{6,2},{1... | collective-permute-start | bytes 1523720 | tf_op jit(solution)/shard_map/ppermute | solution.py:410
  61.7 0.0 copy-done.13
  61.7 0.1 broadcast_in_dim.15.refs_10_
  61.7 0.0 copy-done
  61.7 0.0 copy-done.2
  61.7 0.0 copy-done.5
  61.8 0.0 copy-done.6
  61.8 0.0 copy-done.1
  61.8 6.2 %finish.3.refs_12_ = bf16[64,32,512]{2,1,0:T(8,128)(2,1)} custom-call(s32[3]{0:T(128)S(1)} %copy-done.6, bf16[31,64,128]{2,1,0:T(8,128)(2,1)S(1)} %add_convert_fusion.1.refs_1_.refs_2_, bf16[31,64,128]{2,1,0:T(8,128)(2,1)S(1)} %add_convert_fusion.1.refs_1_.refs_2_, bf16[16,128,128]{2,1,0:T(8,128)(2,1)S(1)} %get-tuple-element.20.refs_3_, ...), custom_call_target="tpu_custom_call" | custom-call | tf_op jit(solution)/shard_map/finish/pallas_call | solution.py:297
  68.0 0.0 collective-permute-done.5
  68.0 1.4 %add_convert_fusion.refs_2_ = bf16[31,64,128]{2,1,0:T(8,128)(2,1)S(1)} fusion(bf16[31,64,128]{2,1,0:T(8,128)(2,1)} %collective-permute-done.5, bf16[31,64,128]{2,1,0:T(8,128)(2,1)} %add_convert_fusion.3), kind=kLoop, calls=%fused_computation.2 | loop fusion | flops 1015808 | bytes 1523712 | tf_op jit(solution)/shard_map/convert_element_type | solution.py:321
  69.4 2.9 %collective-permute-start.6 = (bf16[31,64,128]{2,1,0:T(8,128)(2,1)S(1)}, bf16[31,64,128]{2,1,0:T(8,128)(2,1)S(1)}, u32[]{:S(2)}, u32[]{:S(2)}) collective-permute-start(bf16[31,64,128]{2,1,0:T(8,128)(2,1)S(1)} %add_convert_fusion.refs_2_), channel_id=1, source_target_pairs={{0,4},{4,0},{8,12},{12,8},{1,5},{5,1},{9,13},{13,9},{2,6},{6,2},{1... | collective-permute-start | bytes 1523720 | tf_op jit(solution)/shard_map/ppermute | solution.py:410
  72.3 0.0 collective-permute-done.7.refs_1_
  72.3 11.8 %finish.4.refs_12_ = bf16[64,32,512]{2,1,0:T(8,128)(2,1)} custom-call(s32[3]{0:T(128)S(1)} %copy-done.6, bf16[31,64,128]{2,1,0:T(8,128)(2,1)S(1)} %collective-permute-done.7.refs_1_, bf16[31,64,128]{2,1,0:T(8,128)(2,1)S(1)} %add_convert_fusion.refs_2_, bf16[16,128,128]{2,1,0:T(8,128)(2,1)S(1)} %get-tuple-element.20.refs_3_, ...), custom_call_target="tpu_custom_call", output_to_operand_aliasing={{}: (12, {})} | custom-call | tf_op jit(solution)/shard_map/finish/pallas_call | solution.py:297
  84.1 0.0 collective-permute-done.6.refs_1_.refs_2_
  84.1 6.2 %finish.5 = bf16[64,32,512]{2,1,0:T(8,128)(2,1)} custom-call(s32[3]{0:T(128)S(1)} %copy-done.6, bf16[31,64,128]{2,1,0:T(8,128)(2,1)S(1)} %collective-permute-done.6.refs_1_.refs_2_, bf16[31,64,128]{2,1,0:T(8,128)(2,1)S(1)} %collective-permute-done.6.refs_1_.refs_2_, ...), custom_call_target="tpu_custom_call", output_to_operand_aliasing={{}: (12, {})} | custom-call | tf_op jit(solution)/shard_map/finish/pallas_call | solution.py:297
  (20 shorter events, 0.2 us)
Async XLA Ops:
  4.1 16.9 %collective-permute-start.3 = (bf16[31,64,128]{2,1,0:T(8,128)(2,1)}, bf16[31,64,128]{2,1,0:T(8,128)(2,1)}, u32[]{:S(2)}, u32[]{:S(2)}) collective-permute-start(bf16[31,64,128]{2,1,0:T(8,128)(2,1)} %get-tuple-element.19), channel_id=1, source_target_pairs={{0,4},{4,0},{8,12},{12,8},{1,5},{5,1},{9,13},{13,9},{2,6},{6,2},{1... | collective-permute-start | bytes 1523720 | tf_op jit(solution)/shard_map/ppermute | solution.py:359
  11.9 3.8 %copy-start.12 = (f32[256]{0:T(256)S(1)}, f32[256]{0:T(256)}, u32[]{:S(2)}) copy-start(f32[256]{0:T(256)} %param.16) | copy-start | bytes 3076
  11.9 3.8 %copy-start.11 = (bf16[64,64]{1,0:T(8,128)(2,1)S(1)}, bf16[64,64]{1,0:T(8,128)(2,1)}, u32[]{:S(2)}) copy-start(bf16[64,64]{1,0:T(8,128)(2,1)} %param.14) | copy-start | bytes 24580
  11.9 4.1 %copy-start.10 = (bf16[64,256]{1,0:T(8,128)(2,1)S(1)}, bf16[64,256]{1,0:T(8,128)(2,1)}, u32[]{:S(2)}) copy-start(bf16[64,256]{1,0:T(8,128)(2,1)} %param.15) | copy-start | bytes 98308
  11.9 4.3 %copy-start.3 = (bf16[2,16,64,64]{3,2,1,0:T(8,128)(2,1)S(1)}, bf16[2,16,64,64]{3,2,1,0:T(8,128)(2,1)}, u32[]{:S(2)}) copy-start(bf16[2,16,64,64]{3,2,1,0:T(8,128)(2,1)} %row_ref.1) | copy-start | bytes 786436
  12.0 6.1 %copy-start.7 = (f32[32,2048]{1,0:T(8,128)S(1)}, f32[32,2048]{1,0:T(8,128)}, u32[]{:S(2)}) copy-start(f32[32,2048]{1,0:T(8,128)} %col_modes.1) | copy-start | bytes 786436
  12.0 6.1 %collective-permute-start.1 = (f32[32,2048]{1,0:T(8,128)}, f32[32,2048]{1,0:T(8,128)}, u32[]{:S(2)}, u32[]{:S(2)}) collective-permute-start(f32[32,2048]{1,0:T(8,128)} %col_modes.1), channel_id=1, source_target_pairs={{0,1},{1,0},{2,3},{3,2},{4,5},{5,4},{6,7},{7,6},{8,9},{9,8},{10,11... | collective-permute-start | bytes 786440 | tf_op jit(solution)/shard_map/ppermute | solution.py:334
  15.7 14.6 %collective-permute-start = (bf16[31,64,128]{2,1,0:T(8,128)(2,1)}, bf16[31,64,128]{2,1,0:T(8,128)(2,1)}, u32[]{:S(2)}, u32[]{:S(2)}) collective-permute-start(bf16[31,64,128]{2,1,0:T(8,128)(2,1)} %get-tuple-element.16), channel_id=1, source_target_pairs={{0,4},{4,0},{8,12},{12,8},{1,5},{5,1},{9,13},{13,9},{2,6},{6,2},{1... | collective-permute-start | bytes 1523720 | tf_op jit(solution)/shard_map/ppermute | solution.py:359
  16.2 1.0 %copy-start.4 = (bf16[2,16,64,64]{3,2,1,0:T(8,128)(2,1)S(1)}, bf16[2,16,64,64]{3,2,1,0:T(8,128)(2,1)}, u32[]{:S(2)}) copy-start(bf16[2,16,64,64]{3,2,1,0:T(8,128)(2,1)} %col_ref.1) | copy-start | bytes 786436
  17.3 3.8 %copy-start.8 = (bf16[31,64,128]{2,1,0:T(8,128)(2,1)S(1)}, bf16[31,64,128]{2,1,0:T(8,128)(2,1)}, u32[]{:S(2)}) copy-start(bf16[31,64,128]{2,1,0:T(8,128)(2,1)} %get-tuple-element.18) | copy-start | bytes 1523716
  17.3 13.1 %copy-start.9 = (bf16[31,64,128]{2,1,0:T(8,128)(2,1)S(1)}, bf16[31,64,128]{2,1,0:T(8,128)(2,1)}, u32[]{:S(2)}) copy-start(bf16[31,64,128]{2,1,0:T(8,128)(2,1)} %get-tuple-element.15) | copy-start | bytes 1523716
  19.1 13.3 %collective-permute-start.2 = (f32[32,2048]{1,0:T(8,128)S(1)}, f32[32,2048]{1,0:T(8,128)S(1)}, u32[]{:S(2)}, u32[]{:S(2)}) collective-permute-start(f32[32,2048]{1,0:T(8,128)S(1)} %add.63), channel_id=1, source_target_pairs={{0,2},{1,3},{2,0},{3,1},{4,6},{5,7},{6,4},{7,5},{8,10},{9,11},{10,... | collective-permute-start | bytes 786440 | tf_op jit(solution)/shard_map/ppermute | solution.py:334
  23.1 32.6 %collective-permute-start.4 = (bf16[31,64,128]{2,1,0:T(8,128)(2,1)}, bf16[31,64,128]{2,1,0:T(8,128)(2,1)}, u32[]{:S(2)}, u32[]{:S(2)}) collective-permute-start(bf16[31,64,128]{2,1,0:T(8,128)(2,1)} %add_convert_fusion.2), channel_id=1, source_target_pairs={{0,12},{12,0},{4,8},{8,4},{1,13},{13,1},{5,9},{9,5},{2,14},{14,2},... | collective-permute-start | bytes 1523720 | tf_op jit(solution)/shard_map/ppermute | solution.py:371
  32.7 35.2 %collective-permute-start.5 = (bf16[31,64,128]{2,1,0:T(8,128)(2,1)}, bf16[31,64,128]{2,1,0:T(8,128)(2,1)}, u32[]{:S(2)}, u32[]{:S(2)}) collective-permute-start(bf16[31,64,128]{2,1,0:T(8,128)(2,1)} %add_convert_fusion.3), channel_id=1, source_target_pairs={{0,12},{12,0},{4,8},{8,4},{1,13},{13,1},{5,9},{9,5},{2,14},{14,2},... | collective-permute-start | bytes 1523720 | tf_op jit(solution)/shard_map/ppermute | solution.py:371
  53.8 7.8 %copy-start.13 = (f32[64]{0:T(128)S(1)}, f32[64]{0:T(128)}, u32[]{:S(2)}) copy-start(f32[64]{0:T(128)} %param.18) | copy-start | bytes 772
  53.8 7.9 %copy-start = (bf16[64,32,512]{2,1,0:T(8,128)(2,1)S(1)}, bf16[64,32,512]{2,1,0:T(8,128)(2,1)}, u32[]{:S(2)}) copy-start(bf16[64,32,512]{2,1,0:T(8,128)(2,1)} %refs_6_.5) | copy-start | bytes 6291460
  53.8 7.9 %copy-start.2 = (bf16[256,256]{1,0:T(8,128)(2,1)S(1)}, bf16[256,256]{1,0:T(8,128)(2,1)}, u32[]{:S(2)}) copy-start(bf16[256,256]{1,0:T(8,128)(2,1)} %constant.51.clone.refs_11_) | copy-start | bytes 393220
  53.8 7.9 %copy-start.5 = (bf16[256,64]{0,1:T(8,128)(2,1)S(1)}, bf16[256,64]{0,1:T(8,128)(2,1)}, u32[]{:S(2)}) copy-start(bf16[256,64]{0,1:T(8,128)(2,1)} %param.17) | copy-start | bytes 98308
  53.8 7.9 %copy-start.6 = (s32[3]{0:T(128)S(1)}, s32[3]{0:T(128)}, u32[]{:S(2)}) copy-start(s32[3]{0:T(128)} %pad_add_fusion.place_ref.refs_0_) | copy-start | bytes 40
  55.2 6.5 %copy-start.1 = (bf16[4,512,512]{2,1,0:T(8,128)(2,1)S(1)}, bf16[4,512,512]{2,1,0:T(8,128)(2,1)}, u32[]{:S(2)}) copy-start(bf16[4,512,512]{2,1,0:T(8,128)(2,1)} %constant.52.clone.refs_4_) | copy-start | bytes 6291460
  57.2 15.1 %collective-permute-start.7 = (bf16[31,64,128]{2,1,0:T(8,128)(2,1)S(1)}, bf16[31,64,128]{2,1,0:T(8,128)(2,1)S(1)}, u32[]{:S(2)}, u32[]{:S(2)}) collective-permute-start(bf16[31,64,128]{2,1,0:T(8,128)(2,1)S(1)} %add_convert_fusion.1.refs_1_.refs_2_), channel_id=1, source_target_pairs={{0,4},{4,0},{8,12},{12,8},{1,5},{5,1},{9,13},{13,9},{2,6},{6,2},{1... | collective-permute-start | bytes 1523720 | tf_op jit(solution)/shard_map/ppermute | solution.py:410
  69.4 14.8 %collective-permute-start.6 = (bf16[31,64,128]{2,1,0:T(8,128)(2,1)S(1)}, bf16[31,64,128]{2,1,0:T(8,128)(2,1)S(1)}, u32[]{:S(2)}, u32[]{:S(2)}) collective-permute-start(bf16[31,64,128]{2,1,0:T(8,128)(2,1)S(1)} %add_convert_fusion.refs_2_), channel_id=1, source_target_pairs={{0,4},{4,0},{8,12},{12,8},{1,5},{5,1},{9,13},{13,9},{2,6},{6,2},{1... | collective-permute-start | bytes 1523720 | tf_op jit(solution)/shard_map/ppermute | solution.py:410
